TPU v7x, 512 devices: a whole 4x4x16 slice. The times are simulated.
512 devices in a mesh: aux: 16 (over z), orb: 32 (over y, x, core).
Axes of the slice: x: 4, y: 4, z: 16, core: 2. Of those that a mesh axis runs over, the one named last changes fastest.
Arguments:
- three_index: bfloat16 [2048, 896, 256], P(('aux', 'orb')), may hold values from -6 to 6
- tile_ids: int32 [512, 14, 4], P(('aux', 'orb')), may hold values from 0 to 14, as said below
- occupied: bfloat16 [896, 384], P('orb'), may hold values from -0.5 to 0.5
Outputs:
- exchange_matrix: float32 [896, 896], P('orb', 'aux')
Inputs may be any that keep to these rules, and one draw needn't show every extreme that they name: `tile_ids`: each row tile's slots list distinct basis tiles first and then 14 in the empty slots; at least one slot is used; the first row tile of every slab uses all 4.
All inputs are finite; a program needn't handle non-finite values.
Results may differ from a plain program's by a relative error of at most 0.0003.
Values may be sent and summed in bfloat16 or wider, within the bound.
No kernel may reach another device: no remote copies, remote signals or barrier semaphores. Data moves between devices by JAX's collectives and lax.ppermute only.
A program may use at most 64 MiB of HBM per device.

v0:
```python
import jax
import jax.numpy as jnp
from jax import lax
from jax.sharding import PartitionSpec as P


def per_device(three_index, tile_ids, occupied):
    p_dev = three_index.shape[0]
    basis = three_index.shape[1]
    keep = tile_ids.shape[2]
    tiles = tile_ids.shape[1]
    width = three_index.shape[2] // keep
    nocc = occupied.shape[1]
    n_orb = lax.axis_size("orb")
    n_aux = lax.axis_size("aux")
    coef_all = lax.all_gather(occupied, "orb", axis=0, tiled=True)
    padded = jnp.concatenate([coef_all, jnp.zeros((width, nocc), coef_all.dtype)], axis=0)
    coef_tiles = padded.reshape(tiles + 1, width, nocc)
    chosen = coef_tiles[tile_ids[0]]
    block = three_index.reshape(p_dev, tiles, width, keep, width)
    half = jnp.einsum("pmrkl,mkli->mrpi", block, chosen, preferred_element_type=jnp.float32)
    depth = p_dev * nocc
    factor = half.reshape(basis, depth)
    group_rows = lax.psum_scatter(
        jnp.dot(
            factor, factor.T, precision=lax.Precision.HIGHEST, preferred_element_type=jnp.float32
        ),
        "orb",
        scatter_dimension=0,
        tiled=True,
    )
    summed = lax.psum_scatter(group_rows, "aux", scatter_dimension=1, tiled=True)
    total_aux = p_dev * n_aux * n_orb
    return summed / jnp.sqrt(jnp.float32(total_aux * nocc))


def solution(mesh):
    return jax.shard_map(
        per_device,
        mesh=mesh,
        in_specs=(P(("aux", "orb"), None, None), P(("aux", "orb"), None, None), P("orb", None)),
        out_specs=P("orb", "aux"),
        check_vma=False,
    )
```

profile of v0, /device:TPU:2, one launch (start us, length us, event | category | flops | bytes accessed | tf_op | source)
XLA Modules:
  0.0 302.4 jit_solution(14666199408800329529)
XLA Ops:
  6.5 0.0 all-reduce.6.cloned.1.call-start
  6.5 27.7 %all-gather = bf16[32,28,384]{2,1,0:T(8,128)(2,1)S(1)} all-gather(bf16[1,28,384]{2,1,0:T(8,128)(2,1)} %bitcast.32), channel_id=1, replica_groups=mesh['aux'=16,'orb'=32] {'orb'}, dimensions={0}, use_global_device_ids=true | all-gather | bytes 709632 | tf_op jit(solution)/shard_map/all_gather | solution.py:16
  34.2 0.1 reshape.50
  34.4 0.7 compare_select_fusion
  35.1 0.1 copy.9
  35.2 0.1 reshape.42
  35.3 6.4 %reshape.38 = bf16[4,14,64,4,64]{4,3,2,1,0:T(4,128)(2,1)} reshape(bf16[4,896,256]{2,1,0:T(8,128)(2,1)} %param.3) | data formatting | bytes 3670016 | tf_op jit(solution)/shard_map/reshape | solution.py:20
  41.7 0.1 concatenate.3
  41.8 1.2 gather_fusion
  43.0 3.2 %fusion.3 = f32[14,64,4,384]{3,1,2,0:T(8,128)S(1)} fusion(bf16[14,4,64,384,1]{3,2,1,4,0:T(8,128)(2,1)S(1)} %bitcast.30, bf16[4,14,64,4,64]{4,3,2,1,0:T(4,128)(2,1)} %reshape.38), kind=kOutput, calls=%fused_computation.3 | convolution fusion | flops 704643072 | bytes 10092544 | tf_op jit(solution)/shard_map/pmrkl,mkli->mrpi/dot_general | solution.py:21
  46.2 3.6 %copy.11 = f32[14,64,4,384]{3,2,1,0:T(4,128)S(1)} copy(f32[14,64,4,384]{3,1,2,0:T(8,128)S(1)} %fusion.3) | data formatting | bytes 11010048 | tf_op jit(solution)/shard_map/pmrkl,mkli->mrpi/transpose | solution.py:21
  49.7 0.4 copy.16
  50.2 17.8 %fusion.6 = f32[896,896]{1,0:T(8,128)S(1)} fusion(f32[896,1536]{1,0:T(8,128)S(1)} %bitcast.31), kind=kOutput, calls=%fused_computation.8 | convolution fusion | flops 14797504512 | bytes 8716288 | tf_op jit(solution)/shard_map/dot_general | solution.py:25
  68.0 72.9 %fusion = f32[32,896]{1,0:T(8,128)S(1)} fusion(f32[896,896]{1,0:T(8,128)S(1)} %fusion.6), kind=kCustom, calls=%all-reduce-scatter | all-reduce-scatter fusion | flops 917505 | bytes 3328000
  140.9 1.9 collective-permute-start
  142.9 1.9 collective-permute-start.1
  144.8 1.3 collective-permute-start.2
  146.1 1.3 collective-permute-start.3
  147.4 1.3 dynamic-slice.6
  149.4 0.4 collective-permute-done.3
  149.8 0.0 collective-permute-done
  149.8 3.1 %collective-permute-done.1 = f32[32,896]{1,0:T(8,128)S(1)} collective-permute-done((f32[32,896]{1,0:T(8,128)S(1)}, f32[32,896]{1,0:T(8,128)S(1)}, u32[]{:S(2)}, u32[]{:S(2)}) %collective-permute-start.1) | collective-permute-done | bytes 114720
  152.9 0.0 collective-permute-done.2
  152.9 0.7 concatenate.4
  153.6 0.7 constant_dynamic-slice_fusion
  154.2 0.0 all-reduce.6.cloned.1.call-update
  154.3 1.3 dynamic-slice.2
  156.2 137.9 %all-reduce.6.cloned.1.call-done = f32[28,896]{1,0:T(8,128)} async-done(((f32[28,896]{1,0:T(8,128)}), f32[28,896]{1,0:T(8,128)}) %all-reduce.6.cloned.1.call-update) | async-done | bytes 100368
  294.1 1.4 dynamic-slice_multiply_fusion
  (2 shorter events, 0.0 us)
Async XLA Ops:
  6.5 287.6 %all-reduce.6.cloned.1.call-start = ((), (), s32[]{:S(2)}) async-start(), calls=%async_computation | async-start | bytes 229376
  140.9 8.8 %collective-permute-start = (f32[32,896]{1,0:T(8,128)S(1)}, f32[32,896]{1,0:T(8,128)S(1)}, u32[]{:S(2)}, u32[]{:S(2)}) collective-permute-start(f32[32,896]{1,0:T(8,128)S(1)} %fusion), channel_id=1, source_target_pairs={{0,1},{1,2},{2,3},{3,4},{4,5},{5,6},{6,7},{7,8},{8,9},{9,10},{10,1... | collective-permute-start | bytes 344072
  142.9 10.0 %collective-permute-start.1 = (f32[32,896]{1,0:T(8,128)S(1)}, f32[32,896]{1,0:T(8,128)S(1)}, u32[]{:S(2)}, u32[]{:S(2)}) collective-permute-start(f32[32,896]{1,0:T(8,128)S(1)} %fusion), channel_id=1, source_target_pairs={{0,2},{1,3},{2,4},{3,5},{4,6},{5,7},{6,8},{7,9},{8,10},{9,11},{10,... | collective-permute-start | bytes 344072
  144.8 8.1 %collective-permute-start.2 = (f32[32,896]{1,0:T(8,128)S(1)}, f32[32,896]{1,0:T(8,128)S(1)}, u32[]{:S(2)}, u32[]{:S(2)}) collective-permute-start(f32[32,896]{1,0:T(8,128)S(1)} %fusion), channel_id=1, source_target_pairs={{0,3},{1,4},{2,5},{3,6},{4,7},{5,8},{6,9},{7,10},{8,11},{9,12},{10... | collective-permute-start | bytes 344072
  146.1 3.6 %collective-permute-start.3 = (f32[28,896]{1,0:T(8,128)S(1)}, f32[28,896]{1,0:T(8,128)S(1)}, u32[]{:S(2)}, u32[]{:S(2)}) collective-permute-start(f32[28,896]{1,0:T(8,128)S(1)} %slice.2), channel_id=1, source_target_pairs={{0,4},{1,5},{2,6},{3,7},{4,8},{5,9},{6,10},{7,11},{8,12},{9,13},{1... | collective-permute-start | bytes 301064
Sparse Core Ops, SparseCore 0:
  154.4 139.6 all-reduce.5
where the time goes:
time: 303 us; the launch traced here: 302 us
  waiting for transfers between devices  141 us (47%)
  blocking collectives  101 us (33%)
  matrix products  21 us (7%)
  local copies, waits for them, and re-layouts  15.9 us (5%)
  between operations  14.8 us (5%)
  starting transfers between devices  6.44 us (2%)
    unnamed x6, waiting for transfers between devices  141 us
    unnamed x1, blocking collectives  72.9 us
    all_gather x1, blocking collectives, per_device(): coef_all = lax.all_gather(occupied, 'orb', axis=0, tiled=True)  27.7 us
    dot_general x1, matrix products, per_device(): jnp.dot(factor, factor.T, precision=lax.Precision.HIGHEST, preferred_elem...  17.8 us
    unnamed x5, starting transfers between devices  6.44 us
    reshape x1, local copies, waits for them, and re-layouts, per_device(): block = three_index.reshape(p_dev, tiles, width, keep, width)  6.43 us
  transfers between devices with their start and end apart: 5, of which 3 were waited for; matrix products, arithmetic and copies ran while one was open for 1% of the time, Pallas kernels for 0%

commit v1 on v0

v1 whole, which is shorter than its diff:
```python
import functools

import jax
import jax.numpy as jnp
from jax import lax
from jax.experimental import pallas as pl
from jax.experimental.pallas import tpu as pltpu
from jax.sharding import PartitionSpec as P

F32 = jnp.float32
BF16 = jnp.bfloat16
CODES = 128.0
TOP = 32767.0
TINY = 1e-30


def column_codes(block):
    largest = jnp.maximum(jnp.max(jnp.abs(block), axis=0, keepdims=True), TINY)
    return jnp.ceil(jnp.log2(largest) * CODES) + 1.0


def quantized(block, rows):
    row = lax.broadcasted_iota(jnp.int32, block.shape, 0)
    block = jnp.where(row < rows, block, 0.0)
    code = column_codes(block)
    scaled = jnp.round(block * (TOP * jnp.exp2(code * (-1.0 / CODES))))
    return jnp.where(row == rows, code, scaled)


def exchange_kernel(
    passes, ids_ref, core_ref, own_ref, sibling_ref, coef_ref, out_ref, half, high, low, mine_high, mine_low, total
):
    p_dev, basis, inner = own_ref.shape
    tiles, keep = ids_ref.shape[1] // 4, 4
    width = basis // tiles
    nocc = coef_ref.shape[1]
    groups, slot, _ = out_ref.shape
    rows = basis // groups // 2
    half[pl.ds(basis, half.shape[0] - basis), :] = jnp.zeros((half.shape[0] - basis, half.shape[1]), F32)
    for slab, ref in enumerate((own_ref, sibling_ref)):
        for t in range(tiles):
            picked = [
                coef_ref[pl.ds(pl.multiple_of(ids_ref[slab, t * keep + k] * width, width), width), :]
                for k in range(keep)
            ]
            chosen = jnp.concatenate(picked, axis=0)
            block = ref[:, pl.ds(t * width, width), :].reshape(p_dev * width, inner)
            product = jnp.dot(block, chosen, preferred_element_type=F32)
            for p in range(p_dev):
                piece = product[p * width : (p + 1) * width]
                where = (pl.ds(t * width, width), pl.ds(p * nocc, nocc))
                half[where] = piece
                top = piece.astype(BF16)
                high[where] = top
                if passes == 3:
                    low[where] = (piece - top.astype(F32)).astype(BF16)
        for core in range(2):

            @pl.when(core_ref[0] == core)
            def _():
                for g in range(groups):
                    piece = half[pl.ds((2 * g + core) * rows, slot), :]
                    top = piece.astype(BF16)
                    mine_high[pl.ds(g * slot, slot), :] = top
                    if passes == 3:
                        mine_low[pl.ds(g * slot, slot), :] = (piece - top.astype(F32)).astype(BF16)

        dims = (((1,), (1,)), ((), ()))
        for start in range(0, basis, 256):
            size = min(256, basis - start)
            cols = pl.ds(start, size)
            part = lax.dot_general(mine_high[...], high[cols, :], dims, preferred_element_type=F32)
            if passes == 3:
                part += lax.dot_general(mine_high[...], low[cols, :], dims, preferred_element_type=F32)
                part += lax.dot_general(mine_low[...], high[cols, :], dims, preferred_element_type=F32)
            if slab == 0:
                total[:, cols] = part
            else:
                total[:, cols] += part
    for g in range(groups):
        block = total[pl.ds(g * slot, slot), :]
        out_ref[g] = quantized(block, rows).astype(jnp.int32).astype(jnp.int16)


def group_sum_kernel(rows, columns, in_ref, out_ref):
    groups, slot, basis = in_ref.shape
    total = jnp.zeros((slot, basis), F32)
    for g in range(groups):
        block = in_ref[g].astype(jnp.int32).astype(F32)
        total += block * (jnp.exp2(block[rows : rows + 1] * (1.0 / CODES)) * (1.0 / TOP))
    coded = quantized(total, rows)
    coded = jnp.concatenate([coded, jnp.zeros((slot, 128), F32)], axis=1)
    lane = lax.broadcasted_iota(jnp.int32, (slot // 2, 128), 1)
    for j in range(out_ref.shape[0]):
        first = j * columns // 128 * 128
        shift = j * columns - first
        window = coded[:, first : first + 256]
        if shift:
            window = pltpu.roll(window, 256 - shift, 1)
        window = window[:, :128]
        lower = pltpu.roll(window[slot // 2 :], 64, 1)
        out_ref[j] = jnp.where(lane < 64, window[: slot // 2], lower).astype(jnp.int32).astype(jnp.int16)


def final_sum_kernel(scale, in_ref, out_ref):
    parts, half_slot, _ = in_ref.shape
    rows, columns = out_ref.shape
    lane = lax.broadcasted_iota(jnp.int32, (1, 128), 1)
    total = jnp.zeros((half_slot, 128), F32)
    for z in range(parts):
        block = in_ref[z].astype(jnp.int32).astype(F32)
        code = block[rows - half_slot : rows - half_slot + 1]
        code = jnp.where(lane < 64, pltpu.roll(code, 64, 1), code)
        total += block * jnp.exp2(code * (1.0 / CODES))
    total = total * (scale / TOP)
    out_ref[0:half_slot, :] = total[:, :columns]
    lower = pltpu.roll(total, 64, 1)
    out_ref[half_slot:rows, :] = lower[: rows - half_slot, :columns]


VMEM = pl.BlockSpec(memory_space=pltpu.VMEM)
SMEM = pl.BlockSpec(memory_space=pltpu.SMEM)


def per_device(passes, three_index, tile_ids, occupied):
    p_dev, basis, inner = three_index.shape
    tiles, keep = tile_ids.shape[1:]
    width = inner // keep
    rows, nocc = occupied.shape
    n_orb = lax.axis_size("orb")
    n_aux = lax.axis_size("aux")
    chips = n_orb // 2
    columns = basis // n_aux
    slot = 32
    me = lax.axis_index("orb")
    core, chip = me % 2, me // 2
    across = [[2 * g + c for g in range(chips)] for c in range(2)]
    pairs = [[2 * g, 2 * g + 1] for g in range(chips)]

    with jax.named_scope("sibling_slab"):
        sibling = lax.ppermute(three_index, "orb", [(i, i ^ 1) for i in range(n_orb)])
    with jax.named_scope("gather_coefficients"):
        ids = tile_ids.reshape(1, tiles * keep)
        tail = jnp.pad(ids.astype(BF16), ((0, slot - rows - 1), (0, nocc - tiles * keep)))
        mine = jnp.concatenate([occupied, tail], axis=0)
        spread = jnp.broadcast_to(mine[None], (chips, slot, nocc))
        same_core = lax.all_to_all(spread, "orb", 0, 0, axis_index_groups=across, tiled=True)
        both = lax.all_gather(same_core, "orb", axis=0, axis_index_groups=pairs)
        coef = both[:, :, :rows].transpose(1, 0, 2, 3).reshape(basis, nocc)
        coef = jnp.concatenate([coef, jnp.zeros((width, nocc), BF16)], axis=0)
        theirs = lax.dynamic_slice(both, (1 - core, chip, rows, 0), (1, 1, 1, tiles * keep))
        ids = jnp.concatenate([ids, theirs.reshape(1, tiles * keep).astype(jnp.int32)], axis=0)

    depth = p_dev * nocc
    with jax.named_scope("exchange"):
        coded = pl.pallas_call(
            functools.partial(exchange_kernel, passes),
            out_shape=jax.ShapeDtypeStruct((chips, slot, basis), jnp.int16),
            in_specs=[SMEM, SMEM, VMEM, VMEM, VMEM],
            out_specs=VMEM,
            scratch_shapes=[
                pltpu.VMEM((basis + 8, depth), F32),
                pltpu.VMEM((basis, depth), BF16),
                pltpu.VMEM((basis, depth), BF16),
                pltpu.VMEM((chips * slot, depth), BF16),
                pltpu.VMEM((chips * slot, depth), BF16),
                pltpu.VMEM((chips * slot, basis), F32),
            ],
            compiler_params=pltpu.CompilerParams(vmem_limit_bytes=48 * 1024 * 1024),
        )(ids, core.reshape(1).astype(jnp.int32), three_index, sibling, coef)
    with jax.named_scope("sum_over_chips"):
        coded = lax.all_to_all(coded, "orb", 0, 0, axis_index_groups=across, tiled=True)
        coded = pl.pallas_call(
            functools.partial(group_sum_kernel, rows, columns),
            out_shape=jax.ShapeDtypeStruct((n_aux, slot // 2, 128), jnp.int16),
            in_specs=[VMEM],
            out_specs=VMEM,
            compiler_params=pltpu.CompilerParams(vmem_limit_bytes=32 * 1024 * 1024),
        )(coded)
    with jax.named_scope("sum_over_aux"):
        coded = lax.all_to_all(coded, "aux", 0, 0, tiled=True)
        total_aux = p_dev * n_aux * n_orb
        return pl.pallas_call(
            functools.partial(final_sum_kernel, float(total_aux * nocc) ** -0.5),
            out_shape=jax.ShapeDtypeStruct((rows, columns), F32),
            in_specs=[VMEM],
            out_specs=VMEM,
        )(coded)


def solution(mesh):
    return jax.shard_map(
        functools.partial(per_device, 3),
        mesh=mesh,
        in_specs=(P(("aux", "orb"), None, None), P(("aux", "orb"), None, None), P("orb", None)),
        out_specs=P("orb", "aux"),
        check_vma=False,
    )
```

time: 303 us -> 92.2 us (0.30)
  the two profiles are of different devices: /device:TPU:2 before, /device:TPU:1 now
where the time goes in v1:
time: 92.2 us; the launch traced here: 91.8 us
  blocking collectives  46.6 us (51%)
  Pallas kernels  18 us (20%)
  starting transfers between devices  12.3 us (13%)
  waiting for transfers between devices  9.93 us (11%)
  local copies, waits for them, and re-layouts  4.01 us (4%)
    all_to_all x1, blocking collectives, per_device(): coded = lax.all_to_all(coded, 'aux', 0, 0, tiled=True)  24.2 us
    all_to_all x1, blocking collectives, per_device(): lax.all_to_all(coded, 'orb', 0, 0, axis_index_groups=across, tiled=True)  19.3 us
    pallas_call x1, Pallas kernels, per_device(): pl.pallas_call(functools.partial(exchange_kernel, passes), out_shape=jax....  15.9 us
    all_to_all x1, waiting for transfers between devices, per_device(): lax.all_to_all(spread, 'orb', 0, 0, axis_index_groups=across, tiled=True)  9.93 us
    ppermute x1, starting transfers between devices, per_device(): lax.ppermute(three_index, 'orb', [(i, i ^ 1) for i in range(n_orb)])  8.78 us
    all_to_all x1, starting transfers between devices, per_device(): lax.all_to_all(spread, 'orb', 0, 0, axis_index_groups=across, tiled=True)  3.55 us
    all_gather x1, blocking collectives, per_device(): both = lax.all_gather(same_core, 'orb', axis=0, axis_index_groups=pairs)  3.07 us
  transfers between devices with their start and end apart: 2, of which 1 were waited for; matrix products, arithmetic and copies ran while one was open for 5% of the time, Pallas kernels for 0%

profile of v1, /device:TPU:1, one launch (start us, length us, event | category | flops | bytes accessed | tf_op | source)
XLA Modules:
  0.0 91.8 jit_solution(9370397834707101967)
XLA Ops:
  0.0 8.8 %collective-permute-start = (bf16[4,896,256]{2,1,0:T(8,128)(2,1)}, bf16[4,896,256]{2,1,0:T(8,128)(2,1)}, u32[]{:S(2)}, u32[]{:S(2)}) collective-permute-start(bf16[4,896,256]{2,1,0:T(8,128)(2,1)} %own_ref.1), channel_id=1, source_target_pairs={{0,1},{1,0},{2,3},{3,2},{4,5},{5,4},{6,7},{7,6},{8,9},{9,8},{10,11... | collective-permute-start | bytes 5505032 | tf_op jit(solution)/shard_map/sibling_slab/ppermute | solution.py:141
  8.8 0.8 copy.9
  9.6 0.1 reshape.37
  9.7 0.8 fusion.1
  10.4 0.8 broadcast_in_dim.2
  11.2 3.6 %all-to-all-start = ((bf16[16,32,384]{2,1,0:T(8,128)(2,1)}), bf16[16,32,384]{2,1,0:T(8,128)(2,1)S(1)}, u32[]{:S(2)}, u32[]{:S(2)}) async-start(bf16[16,32,384]{2,1,0:T(8,128)(2,1)} %broadcast_in_dim.2), calls=%async_computation | async-start | bytes 786432 | tf_op jit(solution)/shard_map/gather_coefficients/all_to_all | solution.py:147
  14.8 9.9 %all-to-all-done = bf16[16,32,384]{2,1,0:T(8,128)(2,1)S(1)} async-done(((bf16[16,32,384]{2,1,0:T(8,128)(2,1)}), bf16[16,32,384]{2,1,0:T(8,128)(2,1)S(1)}, u32[]{:S(2)}, u32[]{:S(2)}) %all-to-all-start) | async-done | bytes 393248 | tf_op jit(solution)/shard_map/gather_coefficients/all_to_all | solution.py:147
  24.7 3.1 %all-gather = bf16[32,32,384]{2,1,0:T(8,128)(2,1)S(1)} all-gather(bf16[16,32,384]{2,1,0:T(8,128)(2,1)S(1)} %all-to-all-done), channel_id=2, replica_groups={{0,1},{2,3},{4,5},{6,7},{8,9},{10,11},{12,13},{14,15},{16,17},{18,19},{..., dimensions={0}, use_global_device_ids=true | all-gather | bytes 1179648 | tf_op jit(solution)/shard_map/gather_coefficients/all_gather | solution.py:148
  27.8 0.1 slice_bitcast_fusion
  27.9 0.1 copy.10
  28.0 0.0 copy-start
  28.0 1.0 %reshape.39 = bf16[896,384]{1,0:T(8,128)(2,1)} reshape(bf16[16,2,28,384]{3,2,1,0:T(8,128)(2,1)S(1)} %copy.10) | data formatting | bytes 1376256 | tf_op jit(solution)/shard_map/gather_coefficients/reshape | solution.py:149
  29.0 1.2 %concatenate.11.coef_ref = bf16[960,384]{1,0:T(8,128)(2,1)S(1)} pad(bf16[896,384]{1,0:T(8,128)(2,1)} %reshape.39, bf16[]{:T(256)} %constant.30.clone.1), padding=0_64x0_0 | pad | bytes 1425410 | tf_op jit(solution)/shard_map/gather_coefficients/concatenate | solution.py:150
  30.2 0.0 collective-permute-done.sibling_ref
  30.2 0.0 copy-done
  30.2 15.9 %exchange.1 = s16[16,32,896]{2,1,0:T(8,128)(2,1)S(1)} custom-call(s32[2,56]{1,0:T(2,128)S(1)} %pad_add_fusion.ids_ref, s32[1]{0:T(128)} %bitcast.2.core_ref, bf16[4,896,256]{2,1,0:T(8,128)(2,1)S(1)} %copy-done, bf16[4,896,256]{2,1,0:T(8,128)(2,1)} %collective-permute-done.sibling_ref, bf16[960,384]{1,0:T(8,128)(2,1)S(1)} %concatenate.11.coef_ref), custom_call_target="tpu_custom_call" | custom-call | tf_op jit(solution)/shard_map/exchange/pallas_call | solution.py:156
  46.1 19.3 %all_to_all.15.in_ref = s16[16,32,896]{2,1,0:T(8,128)(2,1)S(1)} all-to-all(s16[16,32,896]{2,1,0:T(8,128)(2,1)S(1)} %exchange.1), channel_id=1, replica_groups={{0,2,4,6,8,10,12,14,16,18,20,22,24,26,28,30},{1,3,5,7,9,11,13,15,17,19,..., dimensions={0} | all-to-all | bytes 1835008 | tf_op jit(solution)/shard_map/sum_over_chips/all_to_all | solution.py:172
  65.5 0.5 sum_over_chips.1
  66.0 24.2 %all_to_all.16.in_ref = s16[16,16,128]{2,1,0:T(8,128)(2,1)} all-to-all(s16[16,16,128]{2,1,0:T(8,128)(2,1)S(1)} %sum_over_chips.1), channel_id=1, replica_groups=mesh['aux'=16,'orb'=32] {'aux'}, dimensions={0} | all-to-all | bytes 131072 | tf_op jit(solution)/shard_map/sum_over_aux/all_to_all | solution.py:181
  90.1 1.6 %sum_over_aux.1 = f32[28,56]{1,0:T(8,128)} custom-call(s16[16,16,128]{2,1,0:T(8,128)(2,1)} %all_to_all.16.in_ref), custom_call_target="tpu_custom_call" | custom-call | tf_op jit(solution)/shard_map/sum_over_aux/pallas_call | solution.py:183
  (3 shorter events, 0.0 us)
Async XLA Ops:
  0.0 30.2 %collective-permute-start = (bf16[4,896,256]{2,1,0:T(8,128)(2,1)}, bf16[4,896,256]{2,1,0:T(8,128)(2,1)}, u32[]{:S(2)}, u32[]{:S(2)}) collective-permute-start(bf16[4,896,256]{2,1,0:T(8,128)(2,1)} %own_ref.1), channel_id=1, source_target_pairs={{0,1},{1,0},{2,3},{3,2},{4,5},{5,4},{6,7},{7,6},{8,9},{9,8},{10,11... | collective-permute-start | bytes 5505032 | tf_op jit(solution)/shard_map/sibling_slab/ppermute | solution.py:141
  11.2 13.5 %all-to-all-start = ((bf16[16,32,384]{2,1,0:T(8,128)(2,1)}), bf16[16,32,384]{2,1,0:T(8,128)(2,1)S(1)}, u32[]{:S(2)}, u32[]{:S(2)}) async-start(bf16[16,32,384]{2,1,0:T(8,128)(2,1)} %broadcast_in_dim.2), calls=%async_computation | async-start | bytes 786432 | tf_op jit(solution)/shard_map/gather_coefficients/all_to_all | solution.py:147
  28.0 2.2 %copy-start = (bf16[4,896,256]{2,1,0:T(8,128)(2,1)S(1)}, bf16[4,896,256]{2,1,0:T(8,128)(2,1)}, u32[]{:S(2)}) copy-start(bf16[4,896,256]{2,1,0:T(8,128)(2,1)} %own_ref.1) | copy-start | bytes 5505028

commit v2 on v1

v2 whole, which is shorter than its diff:
```python
import functools

import jax
import jax.numpy as jnp
from jax import lax
from jax.experimental import pallas as pl
from jax.experimental.pallas import tpu as pltpu
from jax.sharding import PartitionSpec as P

F32 = jnp.float32
BF16 = jnp.bfloat16
CODES = 128.0
TOP = 32767.0
TINY = 1e-30
FIRST_CHIP = 10
FIRST_AUX = 8


def column_codes(block):
    largest = jnp.maximum(jnp.max(jnp.abs(block), axis=0, keepdims=True), TINY)
    return jnp.ceil(jnp.log2(largest) * CODES) + 1.0


def quantized(block, rows):
    row = lax.broadcasted_iota(jnp.int32, block.shape, 0)
    block = jnp.where(row < rows, block, 0.0)
    code = column_codes(block)
    scaled = jnp.round(block * (TOP * jnp.exp2(code * (-1.0 / CODES))))
    return jnp.where(row == rows, code, scaled)


def spread_kernel(ids_ref, occupied_ref, out_ref, block):
    groups = out_ref.shape[0]
    rows, nocc = occupied_ref.shape
    keep, tiles = ids_ref.shape
    block[...] = jnp.zeros(block.shape, F32)
    block[pl.ds(0, rows), :] = occupied_ref[...].astype(F32)
    block[pl.ds(rows, keep), pl.ds(0, tiles)] = ids_ref[...].astype(F32)
    value = block[...].astype(BF16)
    for g in range(groups):
        out_ref[g] = value


def exchange_kernel(first, ids_ref, core_ref, own_ref, sibling_ref, both_ref, out_ref, sibling, coef, half, mine, arrived):
    p_dev, basis, inner = own_ref.shape
    groups = out_ref.shape[0]
    keep, tiles = ids_ref.shape[0] // 2, ids_ref.shape[1]
    width = basis // tiles
    nocc = both_ref.shape[3]
    rows = basis // groups // 2
    copy = pltpu.make_async_copy(sibling_ref, sibling, arrived)
    copy.start()
    for g in range(groups):
        for core in range(2):
            chip = (g + first) % groups
            coef[pl.ds((2 * chip + core) * rows, rows), :] = both_ref[core, g, pl.ds(0, rows), :]
    coef[pl.ds(basis, width), :] = jnp.zeros((width, nocc), BF16)
    for slab, ref in enumerate((own_ref, sibling)):
        if slab == 1:
            copy.wait()
        for t in range(tiles):
            picked = [
                coef[pl.ds(pl.multiple_of(ids_ref[slab * keep + k, t] * width, width), width), :] for k in range(keep)
            ]
            block = ref[:, pl.ds(t * width, width), :].reshape(p_dev * width, inner)
            product = jnp.dot(block, jnp.concatenate(picked, axis=0), preferred_element_type=F32).astype(BF16)
            for p in range(p_dev):
                where = (pl.ds(t * width, width), pl.ds((slab * p_dev + p) * nocc, nocc))
                half[where] = product[p * width : (p + 1) * width]
    for core in range(2):

        @pl.when(core_ref[0] == core)
        def _():
            for g in range(groups):
                chip = (g + first) % groups
                mine[pl.ds(g * rows, rows), :] = half[pl.ds((2 * chip + core) * rows, rows), :]

    for start in range(0, basis, 256):
        size = min(256, basis - start)
        part = lax.dot_general(
            mine[...], half[pl.ds(start, size), :], (((1,), (1,)), ((), ())), preferred_element_type=F32
        )
        for g in range(groups):
            block = part[g * rows : (g + 1) * rows]
            block = jnp.concatenate([block, jnp.zeros((out_ref.shape[1] - rows, size), F32)], axis=0)
            out_ref[g, :, pl.ds(start, size)] = quantized(block, rows).astype(jnp.int32).astype(jnp.int16)


def group_sum_kernel(first, rows, columns, in_ref, out_ref):
    groups, slot, basis = in_ref.shape
    total = jnp.zeros((slot, basis), F32)
    for g in range(groups):
        block = in_ref[g].astype(jnp.int32).astype(F32)
        total += block * (jnp.exp2(block[rows : rows + 1] * (1.0 / CODES)) * (1.0 / TOP))
    coded = quantized(total, rows)
    coded = jnp.concatenate([coded, jnp.zeros((slot, 128), F32)], axis=1)
    lane = lax.broadcasted_iota(jnp.int32, (slot // 2, 128), 1)
    for j in range(out_ref.shape[0]):
        start = (j + first) % out_ref.shape[0] * columns
        base = start // 128 * 128
        shift = start - base
        window = coded[:, base : base + 256]
        if shift:
            window = pltpu.roll(window, 256 - shift, 1)
        window = window[:, :128]
        lower = pltpu.roll(window[slot // 2 :], 64, 1)
        out_ref[j] = jnp.where(lane < 64, window[: slot // 2], lower).astype(jnp.int32).astype(jnp.int16)


def final_sum_kernel(scale, in_ref, out_ref):
    parts, half_slot, _ = in_ref.shape
    rows, columns = out_ref.shape
    lane = lax.broadcasted_iota(jnp.int32, (1, 128), 1)
    total = jnp.zeros((half_slot, 128), F32)
    for z in range(parts):
        block = in_ref[z].astype(jnp.int32).astype(F32)
        code = block[rows - half_slot : rows - half_slot + 1]
        code = jnp.where(lane < 64, pltpu.roll(code, 64, 1), code)
        total += block * jnp.exp2(code * (1.0 / CODES))
    total = total * (scale / TOP)
    out_ref[0:half_slot, :] = total[:, :columns]
    lower = pltpu.roll(total, 64, 1)
    out_ref[half_slot:rows, :] = lower[: rows - half_slot, :columns]


VMEM = pl.BlockSpec(memory_space=pltpu.VMEM)
SMEM = pl.BlockSpec(memory_space=pltpu.SMEM)


def per_device(three_index, tile_ids, occupied):
    p_dev, basis, inner = three_index.shape
    tiles, keep = tile_ids.shape[1:]
    width = inner // keep
    rows, nocc = occupied.shape
    n_orb = lax.axis_size("orb")
    n_aux = lax.axis_size("aux")
    chips = n_orb // 2
    columns = basis // n_aux
    slot = 32
    me = lax.axis_index("orb")
    core, chip = me % 2, me // 2
    across = [[2 * ((g + FIRST_CHIP) % chips) + c for g in range(chips)] for c in range(2)]
    along = [[(z + FIRST_AUX) % n_aux for z in range(n_aux)]]
    pairs = [[2 * g, 2 * g + 1] for g in range(chips)]

    with jax.named_scope("spread_coefficients"):
        ids = tile_ids[0].T
        spread = pl.pallas_call(
            spread_kernel,
            out_shape=jax.ShapeDtypeStruct((chips, slot, nocc), BF16),
            in_specs=[VMEM, VMEM],
            out_specs=VMEM,
            scratch_shapes=[pltpu.VMEM((slot, nocc), F32)],
            compiler_params=pltpu.CompilerParams(vmem_limit_bytes=4 * 1024 * 1024),
        )(ids, occupied)
    with jax.named_scope("sibling_slab"):
        spread, slab = lax.optimization_barrier((spread, three_index))
        sibling = lax.ppermute(slab, "orb", [(i, i ^ 1) for i in range(n_orb)])
    with jax.named_scope("gather_coefficients"):
        same_core = lax.all_to_all(spread, "orb", 0, 0, axis_index_groups=across, tiled=True)
        both = lax.all_gather(same_core, "orb", axis=0, axis_index_groups=pairs)
        theirs = lax.dynamic_slice(both, (1 - core, (chip + chips - FIRST_CHIP) % chips, rows, 0), (1, 1, keep, tiles))
        ids = jnp.concatenate([ids, theirs.reshape(keep, tiles).astype(jnp.int32)], axis=0)

    depth = 2 * p_dev * nocc
    with jax.named_scope("exchange"):
        coded = pl.pallas_call(
            functools.partial(exchange_kernel, FIRST_CHIP),
            out_shape=jax.ShapeDtypeStruct((chips, slot, basis), jnp.int16),
            in_specs=[SMEM, SMEM, VMEM, pl.BlockSpec(memory_space=pl.ANY), VMEM],
            out_specs=VMEM,
            scratch_shapes=[
                pltpu.VMEM(three_index.shape, BF16),
                pltpu.VMEM((basis + width, nocc), BF16),
                pltpu.VMEM((basis, depth), BF16),
                pltpu.VMEM((chips * rows, depth), BF16),
                pltpu.SemaphoreType.DMA,
            ],
            compiler_params=pltpu.CompilerParams(vmem_limit_bytes=32 * 1024 * 1024),
        )(ids, core.reshape(1).astype(jnp.int32), three_index, sibling, both)
    with jax.named_scope("sum_over_chips"):
        coded = lax.all_to_all(coded, "orb", 0, 0, axis_index_groups=across, tiled=True)
        coded = pl.pallas_call(
            functools.partial(group_sum_kernel, FIRST_AUX, rows, columns),
            out_shape=jax.ShapeDtypeStruct((n_aux, slot // 2, 128), jnp.int16),
            in_specs=[VMEM],
            out_specs=VMEM,
            compiler_params=pltpu.CompilerParams(vmem_limit_bytes=8 * 1024 * 1024),
        )(coded)
    with jax.named_scope("sum_over_aux"):
        coded = lax.all_to_all(coded, "aux", 0, 0, axis_index_groups=along, tiled=True)
        total_aux = p_dev * n_aux * n_orb
        return pl.pallas_call(
            functools.partial(final_sum_kernel, float(total_aux * nocc) ** -0.5),
            out_shape=jax.ShapeDtypeStruct((rows, columns), F32),
            in_specs=[VMEM],
            out_specs=VMEM,
            compiler_params=pltpu.CompilerParams(vmem_limit_bytes=4 * 1024 * 1024),
        )(coded)


def solution(mesh):
    return jax.shard_map(
        per_device,
        mesh=mesh,
        in_specs=(P(("aux", "orb"), None, None), P(("aux", "orb"), None, None), P("orb", None)),
        out_specs=P("orb", "aux"),
        check_vma=False,
    )
```

time: 92.2 us -> 72.2 us (0.78)
  Pallas kernels: 18 us -> 10.1 us
  blocking collectives: 46.6 us -> 38.7 us
  waiting for transfers between devices: 9.93 us -> 5.61 us
  starting transfers between devices: 12.3 us -> 15.5 us
  local copies, waits for them, and re-layouts: 4.01 us -> 1.56 us
    pallas_call x2 -> x3, Pallas kernels: 16.4 us -> 9.31 us  [the longest x1 7.96 us: per_device(): pl.pallas_call(functools.partial(exchange_kernel, FIRST_CHIP), out_shape=...]
    all_to_all x1, blocking collectives: 24.2 us -> 18 us  [per_device(): lax.all_to_all(coded, 'aux', 0, 0, axis_index_groups=along, tiled=True)]
    all_to_all x1, waiting for transfers between devices: 9.93 us -> 5.61 us  [per_device(): lax.all_to_all(spread, 'orb', 0, 0, axis_index_groups=across, tiled=True)]
    all_to_all x1, starting transfers between devices: 3.55 us -> 6.68 us  [per_device(): lax.all_to_all(spread, 'orb', 0, 0, axis_index_groups=across, tiled=True)]
    all_to_all x1, blocking collectives: 19.3 us -> 18 us  [per_device(): lax.all_to_all(coded, 'orb', 0, 0, axis_index_groups=across, tiled=True)]
    concatenate x1 -> x0, local copies, waits for them, and re-layouts: 1.17 us -> none  [per_device(): coef = jnp.concatenate([coef, jnp.zeros((width, nocc), BF16)], axis=0)]
    reshape x2 -> x0, local copies, waits for them, and re-layouts: 1.06 us -> none  [the longest x1 0.98 us: per_device(): coef = both[:, :, :rows].transpose(1, 0, 2, 3).reshape(basis, nocc)]
  transfers between devices with their start and end apart: 2 -> 2, of which waited for: 1 -> 1; matrix products, arithmetic and copies ran while one was open for 5% -> 0% of each run, Pallas kernels for 0% -> 0%
where the time goes in v2:
time: 72.2 us; the launch traced here: 71.5 us
  blocking collectives  38.7 us (54%)
  starting transfers between devices  15.5 us (21%)
  Pallas kernels  10.1 us (14%)
  waiting for transfers between devices  5.61 us (8%)
  local copies, waits for them, and re-layouts  1.56 us (2%)
    all_to_all x1, blocking collectives, per_device(): lax.all_to_all(coded, 'aux', 0, 0, axis_index_groups=along, tiled=True)  18 us
    all_to_all x1, blocking collectives, per_device(): lax.all_to_all(coded, 'orb', 0, 0, axis_index_groups=across, tiled=True)  18 us
    ppermute x1, starting transfers between devices, per_device(): sibling = lax.ppermute(slab, 'orb', [(i, i ^ 1) for i in range(n_orb)])  8.78 us
    pallas_call x1, Pallas kernels, per_device(): pl.pallas_call(functools.partial(exchange_kernel, FIRST_CHIP), out_shape=...  7.96 us
    all_to_all x1, starting transfers between devices, per_device(): lax.all_to_all(spread, 'orb', 0, 0, axis_index_groups=across, tiled=True)  6.68 us
    all_to_all x1, waiting for transfers between devices, per_device(): lax.all_to_all(spread, 'orb', 0, 0, axis_index_groups=across, tiled=True)  5.61 us
    all_gather x1, blocking collectives, per_device(): both = lax.all_gather(same_core, 'orb', axis=0, axis_index_groups=pairs)  2.72 us
    unnamed x8, local copies, waits for them, and re-layouts  1.56 us
  transfers between devices with their start and end apart: 2, of which 1 were waited for; matrix products, arithmetic and copies ran while one was open for 0% of the time, Pallas kernels for 0%

profile of v2, /device:TPU:1, one launch (start us, length us, event | category | flops | bytes accessed | tf_op | source)
XLA Modules:
  0.0 71.5 jit_solution(2864907988078678891)
XLA Ops:
  0.0 0.0 copy-start
  0.0 0.0 copy-start.1
  0.0 0.9 %copy-done.1 = bf16[28,384]{1,0:T(8,128)(2,1)S(1)} copy-done((bf16[28,384]{1,0:T(8,128)(2,1)S(1)}, bf16[28,384]{1,0:T(8,128)(2,1)}, u32[]{:S(2)}) %copy-start.1) | copy-done | bytes 21528
  0.9 0.0 copy-start.2
  0.9 0.7 copy-done.2
  1.6 0.0 copy-start.3
  1.6 0.8 %spread_coefficients.1 = bf16[16,32,384]{2,1,0:T(8,128)(2,1)} custom-call(s32[4,14]{1,0:T(4,128)S(1)} %bitcast.10, bf16[28,384]{1,0:T(8,128)(2,1)S(1)} %copy-done.1), custom_call_target="tpu_custom_call" | custom-call | tf_op jit(solution)/shard_map/spread_coefficients/pallas_call | solution.py:148
  2.4 8.8 %collective-permute-start = (bf16[4,896,256]{2,1,0:T(8,128)(2,1)}, bf16[4,896,256]{2,1,0:T(8,128)(2,1)}, u32[]{:S(2)}, u32[]{:S(2)}) collective-permute-start(bf16[4,896,256]{2,1,0:T(8,128)(2,1)} %own_ref.1), channel_id=1, source_target_pairs={{0,1},{1,0},{2,3},{3,2},{4,5},{5,4},{6,7},{7,6},{8,9},{9,8},{10,11... | collective-permute-start | bytes 5505032 | tf_op jit(solution)/shard_map/sibling_slab/ppermute | solution.py:158
  11.1 6.7 %all-to-all-start = ((bf16[16,32,384]{2,1,0:T(8,128)(2,1)}), bf16[16,32,384]{2,1,0:T(8,128)(2,1)S(1)}, u32[]{:S(2)}, u32[]{:S(2)}) async-start(bf16[16,32,384]{2,1,0:T(8,128)(2,1)} %spread_coefficients.1), calls=%async_computation | async-start | bytes 786432 | tf_op jit(solution)/shard_map/gather_coefficients/all_to_all | solution.py:160
  17.8 5.6 %all-to-all-done = bf16[16,32,384]{2,1,0:T(8,128)(2,1)S(1)} async-done(((bf16[16,32,384]{2,1,0:T(8,128)(2,1)}), bf16[16,32,384]{2,1,0:T(8,128)(2,1)S(1)}, u32[]{:S(2)}, u32[]{:S(2)}) %all-to-all-start) | async-done | bytes 393248 | tf_op jit(solution)/shard_map/gather_coefficients/all_to_all | solution.py:160
  23.4 2.7 %all-gather = bf16[32,32,384]{2,1,0:T(8,128)(2,1)S(1)} all-gather(bf16[16,32,384]{2,1,0:T(8,128)(2,1)S(1)} %all-to-all-done), channel_id=2, replica_groups={{0,1},{2,3},{4,5},{6,7},{8,9},{10,11},{12,13},{14,15},{16,17},{18,19},{..., dimensions={0}, use_global_device_ids=true | all-gather | bytes 1179648 | tf_op jit(solution)/shard_map/gather_coefficients/all_gather | solution.py:161
  26.2 0.0 copy-done.3
  26.2 0.0 collective-permute-done.sibling_ref
  26.2 0.0 copy-done
  26.2 8.0 %exchange.1 = s16[16,32,896]{2,1,0:T(8,128)(2,1)S(1)} custom-call(s32[8,14]{1,0:T(8,128)S(1)} %pad_add_fusion.ids_ref, s32[1]{0:T(128)} %bitcast.5.core_ref, bf16[4,896,256]{2,1,0:T(8,128)(2,1)S(1)} %copy-done, bf16[4,896,256]{2,1,0:T(8,128)(2,1)} %collective-permute-done.sibling_ref, bf16[2,16,32,384]{3,2,1,0:T(8,128)(2,1)S(1)} %bitcast.9), custom_call_target="tpu_custom_call" | custom-call | tf_op jit(solution)/shard_map/exchange/pallas_call | solution.py:167
  34.2 18.0 %all_to_all.15.in_ref = s16[16,32,896]{2,1,0:T(8,128)(2,1)S(1)} all-to-all(s16[16,32,896]{2,1,0:T(8,128)(2,1)S(1)} %exchange.1), channel_id=1, replica_groups={{20,22,24,26,28,30,0,2,4,6,8,10,12,14,16,18},{21,23,25,27,29,31,1,3,5,7..., dimensions={0} | all-to-all | bytes 1835008 | tf_op jit(solution)/shard_map/sum_over_chips/all_to_all | solution.py:182
  52.2 0.6 sum_over_chips.1
  52.7 18.0 %all_to_all.16.in_ref = s16[16,16,128]{2,1,0:T(8,128)(2,1)S(1)} all-to-all(s16[16,16,128]{2,1,0:T(8,128)(2,1)S(1)} %sum_over_chips.1), channel_id=1, replica_groups={{256,288,320,352,384,416,448,480,0,32,64,96,128,160,192,224},{257,289,3..., dimensions={0} | all-to-all | bytes 131072 | tf_op jit(solution)/shard_map/sum_over_aux/all_to_all | solution.py:191
  70.7 0.8 %sum_over_aux.1 = f32[28,56]{1,0:T(8,128)} custom-call(s16[16,16,128]{2,1,0:T(8,128)(2,1)S(1)} %all_to_all.16.in_ref), custom_call_target="tpu_custom_call" | custom-call | tf_op jit(solution)/shard_map/sum_over_aux/pallas_call | solution.py:193
  (2 shorter events, 0.0 us)
Async XLA Ops:
  0.0 26.2 %copy-start = (bf16[4,896,256]{2,1,0:T(8,128)(2,1)S(1)}, bf16[4,896,256]{2,1,0:T(8,128)(2,1)}, u32[]{:S(2)}) copy-start(bf16[4,896,256]{2,1,0:T(8,128)(2,1)} %own_ref.1) | copy-start | bytes 5505028
  0.0 0.9 %copy-start.1 = (bf16[28,384]{1,0:T(8,128)(2,1)S(1)}, bf16[28,384]{1,0:T(8,128)(2,1)}, u32[]{:S(2)}) copy-start(bf16[28,384]{1,0:T(8,128)(2,1)} %occupied_ref.1) | copy-start | bytes 64516
  0.9 0.7 copy-start.2
  1.6 24.6 %copy-start.3 = (s32[1,14,4]{1,2,0:T(4,128)S(1)}, s32[1,14,4]{1,2,0:T(4,128)}, u32[]{:S(2)}) copy-start(s32[1,14,4]{1,2,0:T(4,128)} %param.4) | copy-start | bytes 676
  2.4 23.8 %collective-permute-start = (bf16[4,896,256]{2,1,0:T(8,128)(2,1)}, bf16[4,896,256]{2,1,0:T(8,128)(2,1)}, u32[]{:S(2)}, u32[]{:S(2)}) collective-permute-start(bf16[4,896,256]{2,1,0:T(8,128)(2,1)} %own_ref.1), channel_id=1, source_target_pairs={{0,1},{1,0},{2,3},{3,2},{4,5},{5,4},{6,7},{7,6},{8,9},{9,8},{10,11... | collective-permute-start | bytes 5505032 | tf_op jit(solution)/shard_map/sibling_slab/ppermute | solution.py:158
  11.1 12.3 %all-to-all-start = ((bf16[16,32,384]{2,1,0:T(8,128)(2,1)}), bf16[16,32,384]{2,1,0:T(8,128)(2,1)S(1)}, u32[]{:S(2)}, u32[]{:S(2)}) async-start(bf16[16,32,384]{2,1,0:T(8,128)(2,1)} %spread_coefficients.1), calls=%async_computation | async-start | bytes 786432 | tf_op jit(solution)/shard_map/gather_coefficients/all_to_all | solution.py:160

commit v3 on v0

v3 whole, which is shorter than its diff:
```python
import functools

import jax
import jax.numpy as jnp
from jax import lax
from jax.experimental import pallas as pl
from jax.experimental.pallas import tpu as pltpu
from jax.sharding import PartitionSpec as P

F32 = jnp.float32
BF16 = jnp.bfloat16
CODES = 128.0
TOP = 32767.0
TINY = 1e-30
FIRST_CHIP = 10
FIRST_AUX = 8


def wire_rows(rows, basis):
    chunks = basis // 128
    return rows * chunks + (chunks + 1) // 2


def stacked(block):
    return jnp.concatenate([block[:, c : c + 128] for c in range(0, block.shape[1], 128)], axis=0)


def coded(block):
    largest = jnp.maximum(jnp.max(jnp.abs(block), axis=0, keepdims=True), TINY)
    code = jnp.ceil(jnp.log2(largest) * CODES) + 1.0
    return jnp.round(block * (TOP * jnp.exp2(code * (-1.0 / CODES)))), code


def scale_of(code):
    return jnp.exp2(code * (1.0 / CODES)) * (1.0 / TOP)


def as_int16(block):
    return block.astype(jnp.int32).astype(jnp.int16)


def as_float(block):
    return block.astype(jnp.int32).astype(F32)


def pieces(rows, basis):
    for start in range(0, basis, 256):
        yield start, start // 128 * rows, rows * min(2, (basis - start) // 128)


def write_piece(out_ref, g, codes, place, first, block, last):
    values, code = coded(block)
    if not last:
        codes[g, pl.ds(place, 1), :] = code
        out_ref[g, pl.ds(first, block.shape[0]), :] = as_int16(values)
    else:
        values = jnp.concatenate([values, codes[g, pl.ds(0, place), :], code], axis=0)
        out_ref[g, pl.ds(first, values.shape[0]), :] = as_int16(values)


def spread_kernel(occupied_ref, out_ref):
    block = occupied_ref[...].astype(F32)
    rest = jnp.zeros((out_ref.shape[1] - block.shape[0], block.shape[1]), F32)
    block = jnp.concatenate([block, rest], axis=0).astype(BF16)
    for g in range(out_ref.shape[0]):
        out_ref[g] = block


def rows_of_core(first, groups, half, core_ref, other, mine):
    rows = mine.shape[0] // groups
    for core in range(2):

        @pl.when(core_ref[0] == core)
        def _():
            for g in range(groups):
                chip = (g + first) % groups
                mine[pl.ds(g * rows, rows), :] = half[pl.ds((2 * chip + (core ^ other)) * rows, rows), :]


def product_chunks(mine, half):
    basis = half.shape[0]
    for start in range(0, basis, 256):
        cols = pl.ds(start, min(256, basis - start))
        yield lax.dot_general(mine[...], half[cols, :], (((1,), (1,)), ((), ())), preferred_element_type=F32)


def half_kernel(first, ids_ref, core_ref, own_ref, both_ref, half_ref, out_ref, coef, mine, codes):
    p_dev, basis, inner = own_ref.shape
    groups = out_ref.shape[0]
    keep, tiles = ids_ref.shape
    width = basis // tiles
    nocc = both_ref.shape[3]
    rows = basis // groups // 2
    for g in range(groups):
        chip = (g + first) % groups
        for core in range(2):
            coef[pl.ds((2 * chip + core) * rows, rows), :] = both_ref[core, g, pl.ds(0, rows), :]
    coef[pl.ds(basis, width), :] = jnp.zeros((width, nocc), BF16)
    for t in range(tiles):
        picked = [coef[pl.ds(pl.multiple_of(ids_ref[k, t] * width, width), width), :] for k in range(keep)]
        block = own_ref[:, pl.ds(t * width, width), :].reshape(p_dev * width, inner)
        product = jnp.dot(block, jnp.concatenate(picked, axis=0), preferred_element_type=F32).astype(BF16)
        for p in range(p_dev):
            half_ref[pl.ds(t * width, width), pl.ds(p * nocc, nocc)] = product[p * width : (p + 1) * width]
    rows_of_core(first, groups, half_ref, core_ref, 1, mine)
    for place, (part, (start, row, _)) in enumerate(zip(product_chunks(mine, half_ref), pieces(rows, basis))):
        for g in range(groups):
            block = stacked(part[g * rows : (g + 1) * rows])
            write_piece(out_ref, g, codes, place, row, block, start + 256 >= basis)


def own_rows_kernel(first, core_ref, half_ref, out_ref, mine):
    groups = out_ref.shape[0]
    basis = half_ref.shape[0]
    rows = basis // groups // 2
    rows_of_core(first, groups, half_ref, core_ref, 0, mine)
    for part, (_, row, size) in zip(product_chunks(mine, half_ref), pieces(rows, basis)):
        for g in range(groups):
            out_ref[g, pl.ds(row, size), :] = stacked(part[g * rows : (g + 1) * rows])


def pair_sum_kernel(rows, basis, part_ref, in_ref, out_ref, codes):
    groups, length, _ = out_ref.shape
    for g in range(groups):
        theirs = as_float(in_ref[g])
        for place, (start, row, size) in enumerate(pieces(rows, basis)):
            code = theirs[rows * (basis // 128) + place :][:1]
            block = part_ref[g, pl.ds(row, size), :] + theirs[row : row + size] * scale_of(code)
            write_piece(out_ref, g, codes, place, row, block, start + 256 >= basis)


def group_sum_kernel(first, rows, columns, in_ref, out_ref):
    groups, length, _ = in_ref.shape
    parts, half_slot, _ = out_ref.shape
    basis = parts * columns
    totals = [0.0 for _ in pieces(rows, basis)]
    for g in range(groups):
        theirs = as_float(in_ref[g])
        for place, (start, row, size) in enumerate(pieces(rows, basis)):
            code = theirs[rows * (basis // 128) + place :][:1]
            totals[place] += theirs[row : row + size] * scale_of(code)
    chunks = [t[c : c + rows] for t in totals for c in range(0, t.shape[0], rows)]
    values, code = coded(jnp.concatenate(chunks, axis=1))
    rest = jnp.broadcast_to(code, (2 * half_slot - rows, basis))
    both = jnp.concatenate([values, rest], axis=0)
    both = jnp.concatenate([both, jnp.zeros((2 * half_slot, 128), F32)], axis=1)
    lane = lax.broadcasted_iota(jnp.int32, (half_slot, 128), 1)
    for j in range(parts):
        start = (j + first) % parts * columns
        base = start // 128 * 128
        shift = start - base
        window = both[:, base : base + 256]
        if shift:
            window = pltpu.roll(window, 256 - shift, 1)
        window = window[:, :128]
        lower = pltpu.roll(window[half_slot:], 64, 1)
        out_ref[j] = as_int16(jnp.where(lane < 64, window[:half_slot], lower))


def final_sum_kernel(scale, in_ref, out_ref):
    parts, half_slot, _ = in_ref.shape
    rows, columns = out_ref.shape
    lane = lax.broadcasted_iota(jnp.int32, (1, 128), 1)
    total = jnp.zeros((half_slot, 128), F32)
    for z in range(parts):
        block = as_float(in_ref[z])
        code = block[rows - half_slot : rows - half_slot + 1]
        code = jnp.where(lane < 64, pltpu.roll(code, 64, 1), code)
        total += block * jnp.exp2(code * (1.0 / CODES))
    total = total * (scale / TOP)
    out_ref[0:half_slot, :] = total[:, :columns]
    lower = pltpu.roll(total, 64, 1)
    out_ref[half_slot:rows, :] = lower[: rows - half_slot, :columns]


VMEM = pl.BlockSpec(memory_space=pltpu.VMEM)
SMEM = pl.BlockSpec(memory_space=pltpu.SMEM)


def per_device(three_index, tile_ids, occupied):
    p_dev, basis, inner = three_index.shape
    tiles, keep = tile_ids.shape[1:]
    width = inner // keep
    rows, nocc = occupied.shape
    n_orb = lax.axis_size("orb")
    n_aux = lax.axis_size("aux")
    chips = n_orb // 2
    columns = basis // n_aux
    slot = 32
    me = lax.axis_index("orb")
    core = me % 2
    across = [[2 * ((g + FIRST_CHIP) % chips) + c for g in range(chips)] for c in range(2)]
    along = [[(z + FIRST_AUX) % n_aux for z in range(n_aux)]]
    pairs = [[2 * g, 2 * g + 1] for g in range(chips)]

    with jax.named_scope("gather_coefficients"):
        spread = pl.pallas_call(
            spread_kernel,
            out_shape=jax.ShapeDtypeStruct((chips, slot, nocc), BF16),
            in_specs=[VMEM],
            out_specs=VMEM,
            compiler_params=pltpu.CompilerParams(vmem_limit_bytes=4 * 1024 * 1024),
        )(occupied)
        same_core = lax.all_to_all(spread, "orb", 0, 0, axis_index_groups=across, tiled=True)
        both = lax.all_gather(same_core, "orb", axis=0, axis_index_groups=pairs)

    depth = p_dev * nocc
    core = core.reshape(1).astype(jnp.int32)
    wire = (chips, wire_rows(rows, basis), 128)
    sent = jax.ShapeDtypeStruct(wire, jnp.int16)
    codes = pltpu.VMEM((chips, 8, 128), F32)
    flops = basis * basis * depth
    with jax.named_scope("half"):
        half, theirs = pl.pallas_call(
            functools.partial(half_kernel, FIRST_CHIP),
            out_shape=(jax.ShapeDtypeStruct((basis, depth), BF16), sent),
            in_specs=[SMEM, SMEM, VMEM, VMEM],
            out_specs=(VMEM, VMEM),
            scratch_shapes=[pltpu.VMEM((basis + width, nocc), BF16), pltpu.VMEM((chips * rows, depth), BF16), codes],
            compiler_params=pltpu.CompilerParams(vmem_limit_bytes=24 * 1024 * 1024),
            cost_estimate=pl.CostEstimate(flops=2 * flops, bytes_accessed=0, transcendentals=0),
        )(tile_ids[0].T, core, three_index, both)
    with jax.named_scope("sibling_rows"):
        theirs = lax.ppermute(theirs, "orb", [(i, i ^ 1) for i in range(n_orb)])
    with jax.named_scope("own_rows"):
        part = pl.pallas_call(
            functools.partial(own_rows_kernel, FIRST_CHIP),
            out_shape=jax.ShapeDtypeStruct(wire, F32),
            in_specs=[SMEM, VMEM],
            out_specs=VMEM,
            scratch_shapes=[pltpu.VMEM((chips * rows, depth), BF16)],
            compiler_params=pltpu.CompilerParams(vmem_limit_bytes=16 * 1024 * 1024),
            cost_estimate=pl.CostEstimate(flops=flops, bytes_accessed=0, transcendentals=0),
        )(core, half)
    with jax.named_scope("pair_sum"):
        sums = pl.pallas_call(
            functools.partial(pair_sum_kernel, rows, basis),
            out_shape=sent,
            in_specs=[VMEM, VMEM],
            out_specs=VMEM,
            scratch_shapes=[codes],
            compiler_params=pltpu.CompilerParams(vmem_limit_bytes=8 * 1024 * 1024),
        )(part, theirs)
    with jax.named_scope("sum_over_chips"):
        sums = lax.all_to_all(sums, "orb", 0, 0, axis_index_groups=across, tiled=True)
        sums = pl.pallas_call(
            functools.partial(group_sum_kernel, FIRST_AUX, rows, columns),
            out_shape=jax.ShapeDtypeStruct((n_aux, slot // 2, 128), jnp.int16),
            in_specs=[VMEM],
            out_specs=VMEM,
            compiler_params=pltpu.CompilerParams(vmem_limit_bytes=8 * 1024 * 1024),
        )(sums)
    with jax.named_scope("sum_over_aux"):
        sums = lax.all_to_all(sums, "aux", 0, 0, axis_index_groups=along, tiled=True)
        total_aux = p_dev * n_aux * n_orb
        return pl.pallas_call(
            functools.partial(final_sum_kernel, float(total_aux * nocc) ** -0.5),
            out_shape=jax.ShapeDtypeStruct((rows, columns), F32),
            in_specs=[VMEM],
            out_specs=VMEM,
            compiler_params=pltpu.CompilerParams(vmem_limit_bytes=4 * 1024 * 1024),
        )(sums)


def solution(mesh):
    return jax.shard_map(
        per_device,
        mesh=mesh,
        in_specs=(P(("aux", "orb"), None, None), P(("aux", "orb"), None, None), P("orb", None)),
        out_specs=P("orb", "aux"),
        check_vma=False,
    )
```

time: 303 us -> 68.2 us (0.23)
  the two profiles are of different devices: /device:TPU:2 before, /device:TPU:1 now
where the time goes in v3:
time: 68.2 us; the launch traced here: 67.6 us
  blocking collectives  43.2 us (63%)
  starting transfers between devices  11.8 us (17%)
  Pallas kernels  8.1 us (12%)
  waiting for transfers between devices  3.72 us (5%)
  local copies, waits for them, and re-layouts  0.74 us (1%)
    all_to_all x1, blocking collectives, per_device(): lax.all_to_all(sums, 'aux', 0, 0, axis_index_groups=along, tiled=True)  18.7 us
    all_to_all x1, blocking collectives, per_device(): lax.all_to_all(sums, 'orb', 0, 0, axis_index_groups=across, tiled=True)  17 us
    all_to_all x1, starting transfers between devices, per_device(): lax.all_to_all(spread, 'orb', 0, 0, axis_index_groups=across, tiled=True)  9.58 us
    all_gather x1, blocking collectives, per_device(): both = lax.all_gather(same_core, 'orb', axis=0, axis_index_groups=pairs)  7.4 us
    pallas_call x1, Pallas kernels, per_device(): pl.pallas_call(functools.partial(half_kernel, FIRST_CHIP), out_shape=(jax...  3.7 us
    all_to_all x1, waiting for transfers between devices, per_device(): lax.all_to_all(spread, 'orb', 0, 0, axis_index_groups=across, tiled=True)  3.53 us
    ppermute x1, starting transfers between devices, per_device(): theirs = lax.ppermute(theirs, 'orb', [(i, i ^ 1) for i in range(n_orb)])  2.27 us
    pallas_call x1, Pallas kernels, per_device(): pl.pallas_call(functools.partial(own_rows_kernel, FIRST_CHIP), out_shape=...  1.75 us
  transfers between devices with their start and end apart: 2, of which 2 were waited for; matrix products, arithmetic and copies ran while one was open for 0% of the time, Pallas kernels for 3%

profile of v3, /device:TPU:1, one launch (start us, length us, event | category | flops | bytes accessed | tf_op | source)
XLA Modules:
  0.0 67.6 jit_solution(5200938100935939699)
XLA Ops:
  0.0 0.0 copy-start
  0.0 0.7 %copy-done = bf16[28,384]{1,0:T(8,128)(2,1)S(1)} copy-done((bf16[28,384]{1,0:T(8,128)(2,1)S(1)}, bf16[28,384]{1,0:T(8,128)(2,1)}, u32[]{:S(2)}) %copy-start) | copy-done | bytes 21528
  0.7 0.0 copy-start.1
  0.7 0.0 copy-start.2
  0.7 0.8 %gather_coefficients.1 = bf16[16,32,384]{2,1,0:T(8,128)(2,1)} custom-call(bf16[28,384]{1,0:T(8,128)(2,1)S(1)} %copy-done), custom_call_target="tpu_custom_call" | custom-call | tf_op jit(solution)/shard_map/gather_coefficients/pallas_call | solution.py:197
  1.5 9.6 %all-to-all-start = ((bf16[16,32,384]{2,1,0:T(8,128)(2,1)}), bf16[16,32,384]{2,1,0:T(8,128)(2,1)S(1)}, u32[]{:S(2)}, u32[]{:S(2)}) async-start(bf16[16,32,384]{2,1,0:T(8,128)(2,1)} %gather_coefficients.1), calls=%async_computation | async-start | bytes 786432 | tf_op jit(solution)/shard_map/gather_coefficients/all_to_all | solution.py:204
  11.1 3.5 %all-to-all-done = bf16[16,32,384]{2,1,0:T(8,128)(2,1)S(1)} async-done(((bf16[16,32,384]{2,1,0:T(8,128)(2,1)}), bf16[16,32,384]{2,1,0:T(8,128)(2,1)S(1)}, u32[]{:S(2)}, u32[]{:S(2)}) %all-to-all-start) | async-done | bytes 393248 | tf_op jit(solution)/shard_map/gather_coefficients/all_to_all | solution.py:204
  14.6 7.4 %all-gather = bf16[32,32,384]{2,1,0:T(8,128)(2,1)S(1)} all-gather(bf16[16,32,384]{2,1,0:T(8,128)(2,1)S(1)} %all-to-all-done), channel_id=2, replica_groups={{0,1},{2,3},{4,5},{6,7},{8,9},{10,11},{12,13},{14,15},{16,17},{18,19},{..., dimensions={0}, use_global_device_ids=true | all-gather | bytes 1179648 | tf_op jit(solution)/shard_map/gather_coefficients/all_gather | solution.py:205
  22.0 0.0 copy-done.1
  22.0 0.0 copy-done.2
  22.0 3.7 %half.1 = (bf16[896,1536]{1,0:T(8,128)(2,1)S(1)}, s16[16,200,128]{2,1,0:T(8,128)(2,1)S(1)}) custom-call(s32[4,14]{1,0:T(4,128)S(1)} %bitcast.6, s32[1]{0:T(128)} %bitcast.core_ref, bf16[4,896,256]{2,1,0:T(8,128)(2,1)S(1)} %copy-done.1, bf16[2,16,32,384]{3,2,1,0:T(8,128)(2,1)S(1)} %bitcast.5), custom_call_target="tpu_custom_call" | custom-call | flops 2466250752 | tf_op jit(solution)/shard_map/half/pallas_call | solution.py:214
  25.8 2.3 %collective-permute-start = (s16[16,200,128]{2,1,0:T(8,128)(2,1)S(1)}, s16[16,200,128]{2,1,0:T(8,128)(2,1)S(1)}, u32[]{:S(2)}, u32[]{:S(2)}) collective-permute-start(s16[16,200,128]{2,1,0:T(8,128)(2,1)S(1)} %get-tuple-element.8), channel_id=1, source_target_pairs={{0,1},{1,0},{2,3},{3,2},{4,5},{5,4},{6,7},{7,6},{8,9},{9,8},{10,11... | collective-permute-start | bytes 2457608 | tf_op jit(solution)/shard_map/sibling_rows/ppermute | solution.py:224
  28.0 1.7 %own_rows.1.part_ref = f32[16,200,128]{2,1,0:T(8,128)S(1)} custom-call(s32[1]{0:T(128)} %bitcast.core_ref, bf16[896,1536]{1,0:T(8,128)(2,1)S(1)} %get-tuple-element.7.half_ref), custom_call_target="tpu_custom_call" | custom-call | flops 1233125376 | tf_op jit(solution)/shard_map/own_rows/pallas_call | solution.py:226
  29.8 0.2 collective-permute-done.in_ref
  30.0 0.6 pair_sum.1
  30.6 17.0 %all_to_all.15.in_ref = s16[16,200,128]{2,1,0:T(8,128)(2,1)S(1)} all-to-all(s16[16,200,128]{2,1,0:T(8,128)(2,1)S(1)} %pair_sum.1), channel_id=1, replica_groups={{20,22,24,26,28,30,0,2,4,6,8,10,12,14,16,18},{21,23,25,27,29,31,1,3,5,7..., dimensions={0} | all-to-all | bytes 1638400 | tf_op jit(solution)/shard_map/sum_over_chips/all_to_all | solution.py:245
  47.6 0.5 sum_over_chips.1
  48.1 18.7 %all_to_all.16.in_ref = s16[16,16,128]{2,1,0:T(8,128)(2,1)S(1)} all-to-all(s16[16,16,128]{2,1,0:T(8,128)(2,1)S(1)} %sum_over_chips.1), channel_id=1, replica_groups={{256,288,320,352,384,416,448,480,0,32,64,96,128,160,192,224},{257,289,3..., dimensions={0} | all-to-all | bytes 131072 | tf_op jit(solution)/shard_map/sum_over_aux/all_to_all | solution.py:254
  66.8 0.8 %sum_over_aux.1 = f32[28,56]{1,0:T(8,128)} custom-call(s16[16,16,128]{2,1,0:T(8,128)(2,1)S(1)} %all_to_all.16.in_ref), custom_call_target="tpu_custom_call" | custom-call | tf_op jit(solution)/shard_map/sum_over_aux/pallas_call | solution.py:256
Async XLA Ops:
  0.0 0.7 %copy-start = (bf16[28,384]{1,0:T(8,128)(2,1)S(1)}, bf16[28,384]{1,0:T(8,128)(2,1)}, u32[]{:S(2)}) copy-start(bf16[28,384]{1,0:T(8,128)(2,1)} %occupied_ref.1) | copy-start | bytes 64516
  0.7 21.3 %copy-start.1 = (bf16[4,896,256]{2,1,0:T(8,128)(2,1)S(1)}, bf16[4,896,256]{2,1,0:T(8,128)(2,1)}, u32[]{:S(2)}) copy-start(bf16[4,896,256]{2,1,0:T(8,128)(2,1)} %own_ref.1) | copy-start | bytes 5505028
  0.7 21.3 %copy-start.2 = (s32[1,14,4]{1,2,0:T(4,128)S(1)}, s32[1,14,4]{1,2,0:T(4,128)}, u32[]{:S(2)}) copy-start(s32[1,14,4]{1,2,0:T(4,128)} %param.4) | copy-start | bytes 676
  1.5 13.1 %all-to-all-start = ((bf16[16,32,384]{2,1,0:T(8,128)(2,1)}), bf16[16,32,384]{2,1,0:T(8,128)(2,1)S(1)}, u32[]{:S(2)}, u32[]{:S(2)}) async-start(bf16[16,32,384]{2,1,0:T(8,128)(2,1)} %gather_coefficients.1), calls=%async_computation | async-start | bytes 786432 | tf_op jit(solution)/shard_map/gather_coefficients/all_to_all | solution.py:204
  25.8 4.2 %collective-permute-start = (s16[16,200,128]{2,1,0:T(8,128)(2,1)S(1)}, s16[16,200,128]{2,1,0:T(8,128)(2,1)S(1)}, u32[]{:S(2)}, u32[]{:S(2)}) collective-permute-start(s16[16,200,128]{2,1,0:T(8,128)(2,1)S(1)} %get-tuple-element.8), channel_id=1, source_target_pairs={{0,1},{1,0},{2,3},{3,2},{4,5},{5,4},{6,7},{7,6},{8,9},{9,8},{10,11... | collective-permute-start | bytes 2457608 | tf_op jit(solution)/shard_map/sibling_rows/ppermute | solution.py:224

commit v4 on v3

--- a/solution.py
+++ b/solution.py
@@ -14,6 +14,7 @@
 TINY = 1e-30
 FIRST_CHIP = 10
 FIRST_AUX = 8
+ORDER_COST = 20_000_000_000
 
 
 def wire_rows(rows, basis):
@@ -58,15 +59,17 @@
         out_ref[g, pl.ds(first, values.shape[0]), :] = as_int16(values)
 
 
-def spread_kernel(occupied_ref, out_ref):
-    block = occupied_ref[...].astype(F32)
-    rest = jnp.zeros((out_ref.shape[1] - block.shape[0], block.shape[1]), F32)
-    block = jnp.concatenate([block, rest], axis=0).astype(BF16)
+def spread_kernel(ids_ref, occupied_ref, out_ref):
+    keep, tiles = ids_ref.shape
+    chunks = stacked(occupied_ref[...].astype(F32))
+    tail = jnp.concatenate([ids_ref[...].astype(F32), jnp.zeros((keep, 128 - tiles), F32)], axis=1)
+    rest = jnp.zeros((out_ref.shape[1] - chunks.shape[0] - keep, 128), F32)
+    block = jnp.concatenate([chunks, tail] + [rest] * (rest.shape[0] > 0), axis=0).astype(BF16)
     for g in range(out_ref.shape[0]):
         out_ref[g] = block
 
 
-def rows_of_core(first, groups, half, core_ref, other, mine):
+def own_rows(first, groups, half, core_ref, mine):
     rows = mine.shape[0] // groups
     for core in range(2):
 
@@ -74,58 +77,57 @@
         def _():
             for g in range(groups):
                 chip = (g + first) % groups
-                mine[pl.ds(g * rows, rows), :] = half[pl.ds((2 * chip + (core ^ other)) * rows, rows), :]
+                mine[pl.ds(g * rows, rows), :] = half[pl.ds((2 * chip + core) * rows, rows), :]
 
 
 def product_chunks(mine, half):
     basis = half.shape[0]
     for start in range(0, basis, 256):
         cols = pl.ds(start, min(256, basis - start))
-        yield lax.dot_general(mine[...], half[cols, :], (((1,), (1,)), ((), ())), preferred_element_type=F32)
-
-
-def half_kernel(first, ids_ref, core_ref, own_ref, both_ref, half_ref, out_ref, coef, mine, codes):
-    p_dev, basis, inner = own_ref.shape
-    groups = out_ref.shape[0]
+        yield cols, lax.dot_general(mine[...], half[cols, :], (((1,), (1,)), ((), ())), preferred_element_type=F32)
+
+
+def half_transform(ids_ref, slab_ref, coef, half, first_column):
+    p_dev, basis, inner = slab_ref.shape
     keep, tiles = ids_ref.shape
     width = basis // tiles
-    nocc = both_ref.shape[3]
+    nocc = coef.shape[1]
+    for t in range(tiles):
+        picked = [coef[pl.ds(pl.multiple_of(ids_ref[k, t] * width, width), width), :] for k in range(keep)]
+        block = slab_ref[:, pl.ds(t * width, width), :].reshape(p_dev * width, inner)
+        product = jnp.dot(block, jnp.concatenate(picked, axis=0), preferred_element_type=F32).astype(BF16)
+        for p in range(p_dev):
+            half[pl.ds(t * width, width), pl.ds(first_column + p * nocc, nocc)] = product[p * width : (p + 1) * width]
+
+
+def hold_kernel(slab_ref, out_ref):
+    for p in range(slab_ref.shape[0]):
+        out_ref[p] = slab_ref[p]
+
+
+def order_kernel(first, basis, both_ref, coef):
+    groups = both_ref.shape[1]
     rows = basis // groups // 2
     for g in range(groups):
         chip = (g + first) % groups
         for core in range(2):
-            coef[pl.ds((2 * chip + core) * rows, rows), :] = both_ref[core, g, pl.ds(0, rows), :]
-    coef[pl.ds(basis, width), :] = jnp.zeros((width, nocc), BF16)
-    for t in range(tiles):
-        picked = [coef[pl.ds(pl.multiple_of(ids_ref[k, t] * width, width), width), :] for k in range(keep)]
-        block = own_ref[:, pl.ds(t * width, width), :].reshape(p_dev * width, inner)
-        product = jnp.dot(block, jnp.concatenate(picked, axis=0), preferred_element_type=F32).astype(BF16)
-        for p in range(p_dev):
-            half_ref[pl.ds(t * width, width), pl.ds(p * nocc, nocc)] = product[p * width : (p + 1) * width]
-    rows_of_core(first, groups, half_ref, core_ref, 1, mine)
-    for place, (part, (start, row, _)) in enumerate(zip(product_chunks(mine, half_ref), pieces(rows, basis))):
+            for c in range(coef.shape[1] // 128):
+                place = (pl.ds((2 * chip + core) * rows, rows), pl.ds(c * 128, 128))
+                coef[place] = both_ref[core, g, pl.ds(c * rows, rows), :]
+    rest = coef.shape[0] - basis
+    coef[pl.ds(basis, rest), :] = jnp.zeros((rest, coef.shape[1]), BF16)
+
+
+def exchange_kernel(first, ids_ref, their_ids_ref, core_ref, coef, own_ref, sibling_ref, out_ref, half, mine, codes):
+    groups = out_ref.shape[0]
+    basis = half.shape[0]
+    rows = basis // groups // 2
+    half_transform(ids_ref, own_ref, coef, half, 0)
+    half_transform(their_ids_ref, sibling_ref, coef, half, half.shape[1] // 2)
+    own_rows(first, groups, half, core_ref, mine)
+    for place, ((cols, part), (start, row, _)) in enumerate(zip(product_chunks(mine, half), pieces(rows, basis))):
         for g in range(groups):
             block = stacked(part[g * rows : (g + 1) * rows])
-            write_piece(out_ref, g, codes, place, row, block, start + 256 >= basis)
-
-
-def own_rows_kernel(first, core_ref, half_ref, out_ref, mine):
-    groups = out_ref.shape[0]
-    basis = half_ref.shape[0]
-    rows = basis // groups // 2
-    rows_of_core(first, groups, half_ref, core_ref, 0, mine)
-    for part, (_, row, size) in zip(product_chunks(mine, half_ref), pieces(rows, basis)):
-        for g in range(groups):
-            out_ref[g, pl.ds(row, size), :] = stacked(part[g * rows : (g + 1) * rows])
-
-
-def pair_sum_kernel(rows, basis, part_ref, in_ref, out_ref, codes):
-    groups, length, _ = out_ref.shape
-    for g in range(groups):
-        theirs = as_float(in_ref[g])
-        for place, (start, row, size) in enumerate(pieces(rows, basis)):
-            code = theirs[rows * (basis // 128) + place :][:1]
-            block = part_ref[g, pl.ds(row, size), :] + theirs[row : row + size] * scale_of(code)
             write_piece(out_ref, g, codes, place, row, block, start + 256 >= basis)
 
 
@@ -188,59 +190,66 @@
     columns = basis // n_aux
     slot = 32
     me = lax.axis_index("orb")
-    core = me % 2
+    core, chip = me % 2, me // 2
     across = [[2 * ((g + FIRST_CHIP) % chips) + c for g in range(chips)] for c in range(2)]
     along = [[(z + FIRST_AUX) % n_aux for z in range(n_aux)]]
     pairs = [[2 * g, 2 * g + 1] for g in range(chips)]
 
     with jax.named_scope("gather_coefficients"):
+        length = rows * nocc // 128 + keep
+        length += -length % 8
+        ids = tile_ids[0].T
         spread = pl.pallas_call(
             spread_kernel,
-            out_shape=jax.ShapeDtypeStruct((chips, slot, nocc), BF16),
-            in_specs=[VMEM],
-            out_specs=VMEM,
-            compiler_params=pltpu.CompilerParams(vmem_limit_bytes=4 * 1024 * 1024),
-        )(occupied)
+            out_shape=jax.ShapeDtypeStruct((chips, length, 128), BF16),
+            in_specs=[VMEM, VMEM],
+            out_specs=VMEM,
+        )(ids, occupied)
+        spread, slab = lax.optimization_barrier((spread, three_index))
+        own = pl.pallas_call(
+            hold_kernel,
+            out_shape=jax.ShapeDtypeStruct(slab.shape, BF16),
+            in_specs=[VMEM],
+            out_specs=VMEM,
+            compiler_params=pltpu.CompilerParams(vmem_limit_bytes=8 * 1024 * 1024),
+        )(slab)
+        own, slab = lax.optimization_barrier((own, slab))
         same_core = lax.all_to_all(spread, "orb", 0, 0, axis_index_groups=across, tiled=True)
         both = lax.all_gather(same_core, "orb", axis=0, axis_index_groups=pairs)
-
-    depth = p_dev * nocc
+        place = (chip + chips - FIRST_CHIP) % chips
+        pair = [
+            lax.dynamic_slice(both, (c, place, rows * nocc // 128, 0), (1, 1, keep, tiles))
+            for c in (core, 1 - core)
+        ]
+        ids, theirs = (i.reshape(keep, tiles).astype(jnp.int32) for i in pair)
+    with jax.named_scope("sibling_slab"):
+        sibling = lax.ppermute(slab, "orb", [(i, i ^ 1) for i in range(n_orb)])
+
+    depth = 2 * p_dev * nocc
     core = core.reshape(1).astype(jnp.int32)
     wire = (chips, wire_rows(rows, basis), 128)
-    sent = jax.ShapeDtypeStruct(wire, jnp.int16)
-    codes = pltpu.VMEM((chips, 8, 128), F32)
-    flops = basis * basis * depth
-    with jax.named_scope("half"):
-        half, theirs = pl.pallas_call(
-            functools.partial(half_kernel, FIRST_CHIP),
-            out_shape=(jax.ShapeDtypeStruct((basis, depth), BF16), sent),
-            in_specs=[SMEM, SMEM, VMEM, VMEM],
-            out_specs=(VMEM, VMEM),
-            scratch_shapes=[pltpu.VMEM((basis + width, nocc), BF16), pltpu.VMEM((chips * rows, depth), BF16), codes],
-            compiler_params=pltpu.CompilerParams(vmem_limit_bytes=24 * 1024 * 1024),
-            cost_estimate=pl.CostEstimate(flops=2 * flops, bytes_accessed=0, transcendentals=0),
-        )(tile_ids[0].T, core, three_index, both)
-    with jax.named_scope("sibling_rows"):
-        theirs = lax.ppermute(theirs, "orb", [(i, i ^ 1) for i in range(n_orb)])
-    with jax.named_scope("own_rows"):
-        part = pl.pallas_call(
-            functools.partial(own_rows_kernel, FIRST_CHIP),
-            out_shape=jax.ShapeDtypeStruct(wire, F32),
-            in_specs=[SMEM, VMEM],
-            out_specs=VMEM,
-            scratch_shapes=[pltpu.VMEM((chips * rows, depth), BF16)],
-            compiler_params=pltpu.CompilerParams(vmem_limit_bytes=16 * 1024 * 1024),
-            cost_estimate=pl.CostEstimate(flops=flops, bytes_accessed=0, transcendentals=0),
-        )(core, half)
-    with jax.named_scope("pair_sum"):
+    with jax.named_scope("order_coefficients"):
+        coef = pl.pallas_call(
+            functools.partial(order_kernel, FIRST_CHIP, basis),
+            out_shape=jax.ShapeDtypeStruct((basis + width, nocc), BF16),
+            in_specs=[VMEM],
+            out_specs=VMEM,
+            compiler_params=pltpu.CompilerParams(vmem_limit_bytes=8 * 1024 * 1024),
+            cost_estimate=pl.CostEstimate(flops=ORDER_COST, bytes_accessed=0, transcendentals=0),
+        )(both)
+    with jax.named_scope("exchange"):
         sums = pl.pallas_call(
-            functools.partial(pair_sum_kernel, rows, basis),
-            out_shape=sent,
-            in_specs=[VMEM, VMEM],
-            out_specs=VMEM,
-            scratch_shapes=[codes],
-            compiler_params=pltpu.CompilerParams(vmem_limit_bytes=8 * 1024 * 1024),
-        )(part, theirs)
+            functools.partial(exchange_kernel, FIRST_CHIP),
+            out_shape=jax.ShapeDtypeStruct(wire, jnp.int16),
+            in_specs=[SMEM, SMEM, SMEM, VMEM, VMEM, VMEM],
+            out_specs=VMEM,
+            scratch_shapes=[
+                pltpu.VMEM((basis, depth), BF16),
+                pltpu.VMEM((chips * rows, depth), BF16),
+                pltpu.VMEM((chips, 8, 128), F32),
+            ],
+            compiler_params=pltpu.CompilerParams(vmem_limit_bytes=12 * 1024 * 1024),
+        )(ids, theirs, core, coef, own, sibling)
     with jax.named_scope("sum_over_chips"):
         sums = lax.all_to_all(sums, "orb", 0, 0, axis_index_groups=across, tiled=True)
         sums = pl.pallas_call(

time: 68.2 us -> 66.7 us (0.978)
  blocking collectives: 43.2 us -> 38.3 us
  starting transfers between devices: 11.8 us -> 16 us
  waiting for transfers between devices: 3.72 us -> 0.01 us
  Pallas kernels: 8.1 us -> 11.7 us
  local copies, waits for them, and re-layouts: 0.74 us -> 0 us
    ppermute x1, starting transfers between devices: 2.27 us -> 6.44 us  [per_device(): sibling = lax.ppermute(slab, 'orb', [(i, i ^ 1) for i in range(n_orb)])]
    pallas_call x4, Pallas kernels: 6.86 us -> 10.4 us  [the longest x1 7.11 us: per_device(): pl.pallas_call(functools.partial(exchange_kernel, FIRST_CHIP), out_shape=...]
    all_gather x1, blocking collectives: 7.4 us -> 3.84 us  [per_device(): both = lax.all_gather(same_core, 'orb', axis=0, axis_index_groups=pairs)]
    all_to_all x1, waiting for transfers between devices: 3.53 us -> 0.01 us  [per_device(): lax.all_to_all(spread, 'orb', 0, 0, axis_index_groups=across, tiled=True)]
    all_to_all x1, blocking collectives: 18.7 us -> 17.8 us  [per_device(): lax.all_to_all(sums, 'aux', 0, 0, axis_index_groups=along, tiled=True)]
    unnamed x6 -> x0, local copies, waits for them, and re-layouts: 0.74 us -> none
  transfers between devices with their start and end apart: 2 -> 2, of which waited for: 2 -> 0; matrix products, arithmetic and copies ran while one was open for 0% -> 0% of each run, Pallas kernels for 3% -> 3%
where the time goes in v4:
time: 66.7 us; the launch traced here: 66.1 us
  blocking collectives  38.3 us (57%)
  starting transfers between devices  16 us (24%)
  Pallas kernels  11.7 us (18%)
    all_to_all x1, blocking collectives, per_device(): lax.all_to_all(sums, 'aux', 0, 0, axis_index_groups=along, tiled=True)  17.8 us
    all_to_all x1, blocking collectives, per_device(): lax.all_to_all(sums, 'orb', 0, 0, axis_index_groups=across, tiled=True)  16.7 us
    all_to_all x1, starting transfers between devices, per_device(): lax.all_to_all(spread, 'orb', 0, 0, axis_index_groups=across, tiled=True)  9.57 us
    pallas_call x1, Pallas kernels, per_device(): pl.pallas_call(functools.partial(exchange_kernel, FIRST_CHIP), out_shape=...  7.11 us
    ppermute x1, starting transfers between devices, per_device(): sibling = lax.ppermute(slab, 'orb', [(i, i ^ 1) for i in range(n_orb)])  6.44 us
    all_gather x1, blocking collectives, per_device(): both = lax.all_gather(same_core, 'orb', axis=0, axis_index_groups=pairs)  3.84 us
    pallas_call x1, Pallas kernels, per_device(): pl.pallas_call(hold_kernel, out_shape=jax.ShapeDtypeStruct(slab.shape, BF...  1.62 us
    pallas_call x1, Pallas kernels, per_device(): pl.pallas_call(spread_kernel, out_shape=jax.ShapeDtypeStruct((chips, leng...  1.53 us
  transfers between devices with their start and end apart: 2, of which 0 were waited for; matrix products, arithmetic and copies ran while one was open for 0% of the time, Pallas kernels for 3%

profile of v4, /device:TPU:1, one launch (start us, length us, event | category | flops | bytes accessed | tf_op | source)
XLA Modules:
  0.0 66.1 jit_solution(4168468164129966991)
XLA Ops:
  0.0 1.5 %gather_coefficients.2 = bf16[16,88,128]{2,1,0:T(8,128)(2,1)} custom-call(s32[4,14]{1,0:T(4,128)} %bitcast.13, bf16[28,384]{1,0:T(8,128)(2,1)} %occupied_ref.1), custom_call_target="tpu_custom_call" | custom-call | tf_op jit(solution)/shard_map/gather_coefficients/pallas_call | solution.py:202
  1.5 9.6 %all-to-all-start = ((bf16[16,88,128]{2,1,0:T(8,128)(2,1)}), bf16[16,88,128]{2,1,0:T(8,128)(2,1)S(1)}, u32[]{:S(2)}, u32[]{:S(2)}) async-start(bf16[16,88,128]{2,1,0:T(8,128)(2,1)} %gather_coefficients.2), calls=%async_computation | async-start | bytes 720896 | tf_op jit(solution)/shard_map/gather_coefficients/all_to_all | solution.py:217
  11.1 1.6 %gather_coefficients.3.own_ref = bf16[4,896,256]{2,1,0:T(8,128)(2,1)S(1)} custom-call(bf16[4,896,256]{2,1,0:T(8,128)(2,1)} %slab_ref), custom_call_target="tpu_custom_call" | custom-call | tf_op jit(solution)/shard_map/gather_coefficients/pallas_call | solution.py:209
  12.7 6.4 %collective-permute-start = (bf16[4,896,256]{2,1,0:T(8,128)(2,1)}, bf16[4,896,256]{2,1,0:T(8,128)(2,1)}, u32[]{:S(2)}, u32[]{:S(2)}) collective-permute-start(bf16[4,896,256]{2,1,0:T(8,128)(2,1)} %slab_ref), channel_id=1, source_target_pairs={{0,1},{1,0},{2,3},{3,2},{4,5},{5,4},{6,7},{7,6},{8,9},{9,8},{10,11... | collective-permute-start | bytes 5505032 | tf_op jit(solution)/shard_map/sibling_slab/ppermute | solution.py:226
  19.2 0.0 all-to-all-done
  19.2 3.8 %all-gather = bf16[32,88,128]{2,1,0:T(8,128)(2,1)S(1)} all-gather(bf16[16,88,128]{2,1,0:T(8,128)(2,1)S(1)} %all-to-all-done), channel_id=2, replica_groups={{0,1},{2,3},{4,5},{6,7},{8,9},{10,11},{12,13},{14,15},{16,17},{18,19},{..., dimensions={0}, use_global_device_ids=true | all-gather | bytes 1081344 | tf_op jit(solution)/shard_map/gather_coefficients/all_gather | solution.py:218
  23.1 0.2 order_coefficients.1.coef
  23.3 0.0 collective-permute-done.sibling_ref
  23.3 7.1 %exchange.1 = s16[16,200,128]{2,1,0:T(8,128)(2,1)S(1)} custom-call(s32[4,14]{1,0:T(4,128)S(1)} %get-tuple-element.14.ids_ref, s32[4,14]{1,0:T(4,128)S(1)} %get-tuple-element.13.their_ids_ref, s32[1]{0:T(128)} %bitcast.5.core_ref, bf16[960,384]{1,0:T(8,128)(2,1)S(1)} %order_coefficients.1.coef, bf16[4,896,256]{2,1,0:T(8,128)(2,1)S(1)} %gather_coefficients.3.own_ref, ...), custom_call_target="tpu_custom_call" | custom-call | tf_op jit(solution)/shard_map/exchange/pallas_call | solution.py:241
  30.4 16.7 %all_to_all.15.in_ref = s16[16,200,128]{2,1,0:T(8,128)(2,1)S(1)} all-to-all(s16[16,200,128]{2,1,0:T(8,128)(2,1)S(1)} %exchange.1), channel_id=1, replica_groups={{20,22,24,26,28,30,0,2,4,6,8,10,12,14,16,18},{21,23,25,27,29,31,1,3,5,7..., dimensions={0} | all-to-all | bytes 1638400 | tf_op jit(solution)/shard_map/sum_over_chips/all_to_all | solution.py:254
  47.1 0.5 sum_over_chips.1
  47.5 17.8 %all_to_all.16.in_ref = s16[16,16,128]{2,1,0:T(8,128)(2,1)S(1)} all-to-all(s16[16,16,128]{2,1,0:T(8,128)(2,1)S(1)} %sum_over_chips.1), channel_id=1, replica_groups={{256,288,320,352,384,416,448,480,0,32,64,96,128,160,192,224},{257,289,3..., dimensions={0} | all-to-all | bytes 131072 | tf_op jit(solution)/shard_map/sum_over_aux/all_to_all | solution.py:263
  65.3 0.8 %sum_over_aux.1 = f32[28,56]{1,0:T(8,128)} custom-call(s16[16,16,128]{2,1,0:T(8,128)(2,1)S(1)} %all_to_all.16.in_ref), custom_call_target="tpu_custom_call" | custom-call | tf_op jit(solution)/shard_map/sum_over_aux/pallas_call | solution.py:265
  (1 shorter events, 0.0 us)
Async XLA Ops:
  1.5 17.7 %all-to-all-start = ((bf16[16,88,128]{2,1,0:T(8,128)(2,1)}), bf16[16,88,128]{2,1,0:T(8,128)(2,1)S(1)}, u32[]{:S(2)}, u32[]{:S(2)}) async-start(bf16[16,88,128]{2,1,0:T(8,128)(2,1)} %gather_coefficients.2), calls=%async_computation | async-start | bytes 720896 | tf_op jit(solution)/shard_map/gather_coefficients/all_to_all | solution.py:217
  12.7 10.5 %collective-permute-start = (bf16[4,896,256]{2,1,0:T(8,128)(2,1)}, bf16[4,896,256]{2,1,0:T(8,128)(2,1)}, u32[]{:S(2)}, u32[]{:S(2)}) collective-permute-start(bf16[4,896,256]{2,1,0:T(8,128)(2,1)} %slab_ref), channel_id=1, source_target_pairs={{0,1},{1,0},{2,3},{3,2},{4,5},{5,4},{6,7},{7,6},{8,9},{9,8},{10,11... | collective-permute-start | bytes 5505032 | tf_op jit(solution)/shard_map/sibling_slab/ppermute | solution.py:226

commit v5 on v4

--- a/solution.py
+++ b/solution.py
@@ -13,7 +13,7 @@
 TOP = 32767.0
 TINY = 1e-30
 FIRST_CHIP = 10
-FIRST_AUX = 8
+FIRST_AUX = 9
 ORDER_COST = 20_000_000_000
 
 

time: 66.7 us -> 66.7 us (level)
  no operation moved by 1% of the time
where the time goes in v5:
time: 66.7 us; the launch traced here: 66 us
  blocking collectives  38.2 us (57%)
  starting transfers between devices  16 us (24%)
  Pallas kernels  11.7 us (18%)
    all_to_all x1, blocking collectives, per_device(): lax.all_to_all(sums, 'aux', 0, 0, axis_index_groups=along, tiled=True)  17.6 us
    all_to_all x1, blocking collectives, per_device(): lax.all_to_all(sums, 'orb', 0, 0, axis_index_groups=across, tiled=True)  16.7 us
    all_to_all x1, starting transfers between devices, per_device(): lax.all_to_all(spread, 'orb', 0, 0, axis_index_groups=across, tiled=True)  9.57 us
    pallas_call x1, Pallas kernels, per_device(): pl.pallas_call(functools.partial(exchange_kernel, FIRST_CHIP), out_shape=...  7.11 us
    ppermute x1, starting transfers between devices, per_device(): sibling = lax.ppermute(slab, 'orb', [(i, i ^ 1) for i in range(n_orb)])  6.44 us
    all_gather x1, blocking collectives, per_device(): both = lax.all_gather(same_core, 'orb', axis=0, axis_index_groups=pairs)  3.84 us
    pallas_call x1, Pallas kernels, per_device(): pl.pallas_call(hold_kernel, out_shape=jax.ShapeDtypeStruct(slab.shape, BF...  1.62 us
    pallas_call x1, Pallas kernels, per_device(): pl.pallas_call(spread_kernel, out_shape=jax.ShapeDtypeStruct((chips, leng...  1.53 us
  transfers between devices with their start and end apart: 2, of which 0 were waited for; matrix products, arithmetic and copies ran while one was open for 0% of the time, Pallas kernels for 3%

profile of v5, /device:TPU:1, one launch (start us, length us, event | category | flops | bytes accessed | tf_op | source)
XLA Modules:
  0.0 66.0 jit_solution(6939914965775459815)
XLA Ops:
  0.0 1.5 %gather_coefficients.2 = bf16[16,88,128]{2,1,0:T(8,128)(2,1)} custom-call(s32[4,14]{1,0:T(4,128)} %bitcast.13, bf16[28,384]{1,0:T(8,128)(2,1)} %occupied_ref.1), custom_call_target="tpu_custom_call" | custom-call | tf_op jit(solution)/shard_map/gather_coefficients/pallas_call | solution.py:202
  1.5 9.6 %all-to-all-start = ((bf16[16,88,128]{2,1,0:T(8,128)(2,1)}), bf16[16,88,128]{2,1,0:T(8,128)(2,1)S(1)}, u32[]{:S(2)}, u32[]{:S(2)}) async-start(bf16[16,88,128]{2,1,0:T(8,128)(2,1)} %gather_coefficients.2), calls=%async_computation | async-start | bytes 720896 | tf_op jit(solution)/shard_map/gather_coefficients/all_to_all | solution.py:217
  11.1 1.6 %gather_coefficients.3.own_ref = bf16[4,896,256]{2,1,0:T(8,128)(2,1)S(1)} custom-call(bf16[4,896,256]{2,1,0:T(8,128)(2,1)} %slab_ref), custom_call_target="tpu_custom_call" | custom-call | tf_op jit(solution)/shard_map/gather_coefficients/pallas_call | solution.py:209
  12.7 6.4 %collective-permute-start = (bf16[4,896,256]{2,1,0:T(8,128)(2,1)}, bf16[4,896,256]{2,1,0:T(8,128)(2,1)}, u32[]{:S(2)}, u32[]{:S(2)}) collective-permute-start(bf16[4,896,256]{2,1,0:T(8,128)(2,1)} %slab_ref), channel_id=1, source_target_pairs={{0,1},{1,0},{2,3},{3,2},{4,5},{5,4},{6,7},{7,6},{8,9},{9,8},{10,11... | collective-permute-start | bytes 5505032 | tf_op jit(solution)/shard_map/sibling_slab/ppermute | solution.py:226
  19.2 0.0 all-to-all-done
  19.2 3.8 %all-gather = bf16[32,88,128]{2,1,0:T(8,128)(2,1)S(1)} all-gather(bf16[16,88,128]{2,1,0:T(8,128)(2,1)S(1)} %all-to-all-done), channel_id=2, replica_groups={{0,1},{2,3},{4,5},{6,7},{8,9},{10,11},{12,13},{14,15},{16,17},{18,19},{..., dimensions={0}, use_global_device_ids=true | all-gather | bytes 1081344 | tf_op jit(solution)/shard_map/gather_coefficients/all_gather | solution.py:218
  23.1 0.2 order_coefficients.1.coef
  23.3 0.0 collective-permute-done.sibling_ref
  23.3 7.1 %exchange.1 = s16[16,200,128]{2,1,0:T(8,128)(2,1)S(1)} custom-call(s32[4,14]{1,0:T(4,128)S(1)} %get-tuple-element.14.ids_ref, s32[4,14]{1,0:T(4,128)S(1)} %get-tuple-element.13.their_ids_ref, s32[1]{0:T(128)} %bitcast.5.core_ref, bf16[960,384]{1,0:T(8,128)(2,1)S(1)} %order_coefficients.1.coef, bf16[4,896,256]{2,1,0:T(8,128)(2,1)S(1)} %gather_coefficients.3.own_ref, ...), custom_call_target="tpu_custom_call" | custom-call | tf_op jit(solution)/shard_map/exchange/pallas_call | solution.py:241
  30.4 16.7 %all_to_all.15.in_ref = s16[16,200,128]{2,1,0:T(8,128)(2,1)S(1)} all-to-all(s16[16,200,128]{2,1,0:T(8,128)(2,1)S(1)} %exchange.1), channel_id=1, replica_groups={{20,22,24,26,28,30,0,2,4,6,8,10,12,14,16,18},{21,23,25,27,29,31,1,3,5,7..., dimensions={0} | all-to-all | bytes 1638400 | tf_op jit(solution)/shard_map/sum_over_chips/all_to_all | solution.py:254
  47.1 0.5 sum_over_chips.1
  47.5 17.6 %all_to_all.16.in_ref = s16[16,16,128]{2,1,0:T(8,128)(2,1)S(1)} all-to-all(s16[16,16,128]{2,1,0:T(8,128)(2,1)S(1)} %sum_over_chips.1), channel_id=1, replica_groups={{288,320,352,384,416,448,480,0,32,64,96,128,160,192,224,256},{289,321,3..., dimensions={0} | all-to-all | bytes 131072 | tf_op jit(solution)/shard_map/sum_over_aux/all_to_all | solution.py:263
  65.2 0.8 %sum_over_aux.1 = f32[28,56]{1,0:T(8,128)} custom-call(s16[16,16,128]{2,1,0:T(8,128)(2,1)S(1)} %all_to_all.16.in_ref), custom_call_target="tpu_custom_call" | custom-call | tf_op jit(solution)/shard_map/sum_over_aux/pallas_call | solution.py:265
  (1 shorter events, 0.0 us)
Async XLA Ops:
  1.5 17.7 %all-to-all-start = ((bf16[16,88,128]{2,1,0:T(8,128)(2,1)}), bf16[16,88,128]{2,1,0:T(8,128)(2,1)S(1)}, u32[]{:S(2)}, u32[]{:S(2)}) async-start(bf16[16,88,128]{2,1,0:T(8,128)(2,1)} %gather_coefficients.2), calls=%async_computation | async-start | bytes 720896 | tf_op jit(solution)/shard_map/gather_coefficients/all_to_all | solution.py:217
  12.7 10.5 %collective-permute-start = (bf16[4,896,256]{2,1,0:T(8,128)(2,1)}, bf16[4,896,256]{2,1,0:T(8,128)(2,1)}, u32[]{:S(2)}, u32[]{:S(2)}) collective-permute-start(bf16[4,896,256]{2,1,0:T(8,128)(2,1)} %slab_ref), channel_id=1, source_target_pairs={{0,1},{1,0},{2,3},{3,2},{4,5},{5,4},{6,7},{7,6},{8,9},{9,8},{10,11... | collective-permute-start | bytes 5505032 | tf_op jit(solution)/shard_map/sibling_slab/ppermute | solution.py:226

commit v6 on v5

--- a/solution.py
+++ b/solution.py
@@ -12,7 +12,7 @@
 CODES = 128.0
 TOP = 32767.0
 TINY = 1e-30
-FIRST_CHIP = 10
+FIRST_CHIP = (14, 10)
 FIRST_AUX = 9
 ORDER_COST = 20_000_000_000
 
@@ -76,7 +76,7 @@
         @pl.when(core_ref[0] == core)
         def _():
             for g in range(groups):
-                chip = (g + first) % groups
+                chip = (g + first[core]) % groups
                 mine[pl.ds(g * rows, rows), :] = half[pl.ds((2 * chip + core) * rows, rows), :]
 
 
@@ -109,8 +109,8 @@
     groups = both_ref.shape[1]
     rows = basis // groups // 2
     for g in range(groups):
-        chip = (g + first) % groups
         for core in range(2):
+            chip = (g + first[core]) % groups
             for c in range(coef.shape[1] // 128):
                 place = (pl.ds((2 * chip + core) * rows, rows), pl.ds(c * 128, 128))
                 coef[place] = both_ref[core, g, pl.ds(c * rows, rows), :]
@@ -191,7 +191,7 @@
     slot = 32
     me = lax.axis_index("orb")
     core, chip = me % 2, me // 2
-    across = [[2 * ((g + FIRST_CHIP) % chips) + c for g in range(chips)] for c in range(2)]
+    across = [[2 * ((g + FIRST_CHIP[c]) % chips) + c for g in range(chips)] for c in range(2)]
     along = [[(z + FIRST_AUX) % n_aux for z in range(n_aux)]]
     pairs = [[2 * g, 2 * g + 1] for g in range(chips)]
 
@@ -216,10 +216,9 @@
         own, slab = lax.optimization_barrier((own, slab))
         same_core = lax.all_to_all(spread, "orb", 0, 0, axis_index_groups=across, tiled=True)
         both = lax.all_gather(same_core, "orb", axis=0, axis_index_groups=pairs)
-        place = (chip + chips - FIRST_CHIP) % chips
         pair = [
             lax.dynamic_slice(both, (c, place, rows * nocc // 128, 0), (1, 1, keep, tiles))
-            for c in (core, 1 - core)
+            for c, place in ((c, (chip + chips - jnp.where(c == 0, *FIRST_CHIP)) % chips) for c in (core, 1 - core))
         ]
         ids, theirs = (i.reshape(keep, tiles).astype(jnp.int32) for i in pair)
     with jax.named_scope("sibling_slab"):

time: 66.7 us -> 66.6 us (level)
  no operation moved by 1% of the time
where the time goes in v6:
time: 66.6 us; the launch traced here: 65.7 us
  blocking collectives  38.1 us (57%)
  starting transfers between devices  15.7 us (24%)
  Pallas kernels  11.7 us (18%)
    all_to_all x1, blocking collectives, per_device(): lax.all_to_all(sums, 'aux', 0, 0, axis_index_groups=along, tiled=True)  17.6 us
    all_to_all x1, blocking collectives, per_device(): lax.all_to_all(sums, 'orb', 0, 0, axis_index_groups=across, tiled=True)  16.7 us
    all_to_all x1, starting transfers between devices, per_device(): lax.all_to_all(spread, 'orb', 0, 0, axis_index_groups=across, tiled=True)  9.57 us
    pallas_call x1, Pallas kernels, per_device(): pl.pallas_call(functools.partial(exchange_kernel, FIRST_CHIP), out_shape=...  7.11 us
    ppermute x1, starting transfers between devices, per_device(): sibling = lax.ppermute(slab, 'orb', [(i, i ^ 1) for i in range(n_orb)])  6.15 us
    all_gather x1, blocking collectives, per_device(): both = lax.all_gather(same_core, 'orb', axis=0, axis_index_groups=pairs)  3.81 us
    pallas_call x1, Pallas kernels, per_device(): pl.pallas_call(hold_kernel, out_shape=jax.ShapeDtypeStruct(slab.shape, BF...  1.62 us
    pallas_call x1, Pallas kernels, per_device(): pl.pallas_call(spread_kernel, out_shape=jax.ShapeDtypeStruct((chips, leng...  1.53 us
  transfers between devices with their start and end apart: 2, of which 0 were waited for; matrix products, arithmetic and copies ran while one was open for 0% of the time, Pallas kernels for 3%

profile of v6, /device:TPU:1, one launch (start us, length us, event | category | flops | bytes accessed | tf_op | source)
XLA Modules:
  0.0 65.7 jit_solution(4186577888826862625)
XLA Ops:
  0.0 1.5 %gather_coefficients.2 = bf16[16,88,128]{2,1,0:T(8,128)(2,1)} custom-call(s32[4,14]{1,0:T(4,128)} %bitcast.13, bf16[28,384]{1,0:T(8,128)(2,1)} %occupied_ref.1), custom_call_target="tpu_custom_call" | custom-call | tf_op jit(solution)/shard_map/gather_coefficients/pallas_call | solution.py:202
  1.5 9.6 %all-to-all-start = ((bf16[16,88,128]{2,1,0:T(8,128)(2,1)}), bf16[16,88,128]{2,1,0:T(8,128)(2,1)S(1)}, u32[]{:S(2)}, u32[]{:S(2)}) async-start(bf16[16,88,128]{2,1,0:T(8,128)(2,1)} %gather_coefficients.2), calls=%async_computation | async-start | bytes 720896 | tf_op jit(solution)/shard_map/gather_coefficients/all_to_all | solution.py:217
  11.1 1.6 %gather_coefficients.3.own_ref = bf16[4,896,256]{2,1,0:T(8,128)(2,1)S(1)} custom-call(bf16[4,896,256]{2,1,0:T(8,128)(2,1)} %slab_ref), custom_call_target="tpu_custom_call" | custom-call | tf_op jit(solution)/shard_map/gather_coefficients/pallas_call | solution.py:209
  12.7 6.1 %collective-permute-start = (bf16[4,896,256]{2,1,0:T(8,128)(2,1)}, bf16[4,896,256]{2,1,0:T(8,128)(2,1)}, u32[]{:S(2)}, u32[]{:S(2)}) collective-permute-start(bf16[4,896,256]{2,1,0:T(8,128)(2,1)} %slab_ref), channel_id=1, source_target_pairs={{0,1},{1,0},{2,3},{3,2},{4,5},{5,4},{6,7},{7,6},{8,9},{9,8},{10,11... | collective-permute-start | bytes 5505032 | tf_op jit(solution)/shard_map/sibling_slab/ppermute | solution.py:225
  19.0 0.0 all-to-all-done
  19.0 3.8 %all-gather = bf16[32,88,128]{2,1,0:T(8,128)(2,1)S(1)} all-gather(bf16[16,88,128]{2,1,0:T(8,128)(2,1)S(1)} %all-to-all-done), channel_id=2, replica_groups={{0,1},{2,3},{4,5},{6,7},{8,9},{10,11},{12,13},{14,15},{16,17},{18,19},{..., dimensions={0}, use_global_device_ids=true | all-gather | bytes 1081344 | tf_op jit(solution)/shard_map/gather_coefficients/all_gather | solution.py:218
  22.8 0.2 order_coefficients.1.coef
  23.0 0.0 collective-permute-done.sibling_ref
  23.0 7.1 %exchange.1 = s16[16,200,128]{2,1,0:T(8,128)(2,1)S(1)} custom-call(s32[4,14]{1,0:T(4,128)S(1)} %get-tuple-element.14.ids_ref, s32[4,14]{1,0:T(4,128)S(1)} %get-tuple-element.13.their_ids_ref, s32[1]{0:T(128)} %bitcast.5.core_ref, bf16[960,384]{1,0:T(8,128)(2,1)S(1)} %order_coefficients.1.coef, bf16[4,896,256]{2,1,0:T(8,128)(2,1)S(1)} %gather_coefficients.3.own_ref, ...), custom_call_target="tpu_custom_call" | custom-call | tf_op jit(solution)/shard_map/exchange/pallas_call | solution.py:240
  30.1 16.7 %all_to_all.15.in_ref = s16[16,200,128]{2,1,0:T(8,128)(2,1)S(1)} all-to-all(s16[16,200,128]{2,1,0:T(8,128)(2,1)S(1)} %exchange.1), channel_id=1, replica_groups={{28,30,0,2,4,6,8,10,12,14,16,18,20,22,24,26},{21,23,25,27,29,31,1,3,5,7..., dimensions={0} | all-to-all | bytes 1638400 | tf_op jit(solution)/shard_map/sum_over_chips/all_to_all | solution.py:253
  46.8 0.5 sum_over_chips.1
  47.2 17.6 %all_to_all.16.in_ref = s16[16,16,128]{2,1,0:T(8,128)(2,1)S(1)} all-to-all(s16[16,16,128]{2,1,0:T(8,128)(2,1)S(1)} %sum_over_chips.1), channel_id=1, replica_groups={{288,320,352,384,416,448,480,0,32,64,96,128,160,192,224,256},{289,321,3..., dimensions={0} | all-to-all | bytes 131072 | tf_op jit(solution)/shard_map/sum_over_aux/all_to_all | solution.py:262
  64.9 0.8 %sum_over_aux.1 = f32[28,56]{1,0:T(8,128)} custom-call(s16[16,16,128]{2,1,0:T(8,128)(2,1)S(1)} %all_to_all.16.in_ref), custom_call_target="tpu_custom_call" | custom-call | tf_op jit(solution)/shard_map/sum_over_aux/pallas_call | solution.py:264
  (1 shorter events, 0.0 us)
Async XLA Ops:
  1.5 17.4 %all-to-all-start = ((bf16[16,88,128]{2,1,0:T(8,128)(2,1)}), bf16[16,88,128]{2,1,0:T(8,128)(2,1)S(1)}, u32[]{:S(2)}, u32[]{:S(2)}) async-start(bf16[16,88,128]{2,1,0:T(8,128)(2,1)} %gather_coefficients.2), calls=%async_computation | async-start | bytes 720896 | tf_op jit(solution)/shard_map/gather_coefficients/all_to_all | solution.py:217
  12.7 10.2 %collective-permute-start = (bf16[4,896,256]{2,1,0:T(8,128)(2,1)}, bf16[4,896,256]{2,1,0:T(8,128)(2,1)}, u32[]{:S(2)}, u32[]{:S(2)}) collective-permute-start(bf16[4,896,256]{2,1,0:T(8,128)(2,1)} %slab_ref), channel_id=1, source_target_pairs={{0,1},{1,0},{2,3},{3,2},{4,5},{5,4},{6,7},{7,6},{8,9},{9,8},{10,11... | collective-permute-start | bytes 5505032 | tf_op jit(solution)/shard_map/sibling_slab/ppermute | solution.py:225
